TPU v7x, 32 devices: a whole 2x2x4 slice. The times are simulated.
32 devices in a mesh: groups: 2 (over x), chol: 16 (over z, y, core).
Axes of the slice: x: 2, y: 2, z: 4, core: 2. Of those that a mesh axis runs over, the one named last changes fastest.
Arguments:
- green: bfloat16 [8, 256, 1024], P('groups', 'chol'), parts along dimension 0, may hold values from -6 to 6
- chol_vecs: bfloat16 [192, 256, 1024], P('chol'), may hold values from -0.15625 to 0.15625, as said below
- cotangent: float32 [8], P('groups'), parts along dimension 0, may hold values from 1536 to 6144
Outputs:
- energy: float32 [8], P('groups'), parts along dimension 0
- grad_green: float32 [8, 256, 1024], P('groups', 'chol'), parts along dimension 0
There are 2 independent parts, one for each index of `groups`. A program takes and returns all parts, laid end to end along the dimension named above; an argument that names none is the same for every part. Nothing has to cross between parts.
Inputs may be any that keep to these rules, and one draw needn't show every extreme that they name: `chol_vecs`: each vector's entries are of order 1024 ** -0.5 times a factor that changes slowly from vector to vector.
All inputs are finite; a program needn't handle non-finite values.
Results may differ from a plain program's by a relative error of at most 0.0029.
Values may be sent and summed in bfloat16 or wider, within the bound.
A program may use at most 64 MiB of HBM per device.

v0:
```python
import jax
import jax.numpy as jnp
from jax import lax
from jax.sharding import PartitionSpec as P


def per_device(green, chol_vecs, cotangent):
    count = chol_vecs.shape[0]
    walkers = green.shape[0]
    occupied = chol_vecs.shape[1]
    basis = chol_vecs.shape[2]
    scale = 1.0 / (occupied * count * lax.axis_size("chol"))
    full_green = lax.all_gather(green, "chol", axis=1, tiled=True)
    per_block = 4
    blocks = chol_vecs.reshape(count // per_block, per_block, occupied, basis)

    def step(carry, lblock):
        energy_acc, grad_acc = carry
        tmat = jnp.einsum("gip,wjp->wgij", lblock, full_green, preferred_element_type=jnp.float32)
        pairs = jnp.einsum("wgij,wgji->w", tmat, tmat)
        thalf = tmat.astype(jnp.bfloat16)
        gpart = jnp.einsum("wgki,gip->wkp", thalf, lblock, preferred_element_type=jnp.float32)
        return ((energy_acc + pairs, grad_acc + gpart), None)

    start = (jnp.zeros((walkers,), jnp.float32), jnp.zeros((walkers, occupied, basis), jnp.float32))
    (energy_part, grad_part), unused = lax.scan(step, start, blocks)
    energy_sum = lax.psum(energy_part, "chol")
    own_rows = lax.psum_scatter(grad_part, "chol", scatter_dimension=1, tiled=True)
    energy = -0.5 * scale * energy_sum
    grad_green = -scale * cotangent[:, None, None] * own_rows
    return (energy, grad_green)


def solution(mesh):
    placed = (P("groups", "chol", None), P("chol", None, None), P("groups"))
    return jax.shard_map(
        per_device,
        mesh=mesh,
        in_specs=placed,
        out_specs=(P("groups"), P("groups", "chol", None)),
        check_vma=False,
    )
```

profile of v0, /device:TPU:0, one launch (start us, length us, event | category | flops | bytes accessed | tf_op | source)
XLA Modules:
  0.0 205.9 jit_solution(18083906804146891945)
XLA Ops:
  7.2 0.0 all-gather.2.cloned.1.call-start
  7.2 0.7 all-gather.2.cloned.1.call-update
  7.9 0.0 reduce-scatter.2.cloned.1.call-start
  8.0 46.4 %all-gather.2.cloned.1.call-done = bf16[4,256,1024]{2,1,0:T(8,128)(2,1)} async-done(((bf16[4,16,1024]{2,1,0:T(8,128)(2,1)}), bf16[4,256,1024]{2,1,0:T(8,128)(2,1)}) %all-gather.2.cloned.1.call-update) | async-done | bytes 2097168 | tf_op jit(solution)/shard_map/all_gather | solution.py:13
  54.3 71.5 %while.13 = (s32[]{:T(128)}, f32[4]{0:T(128)S(1)}, f32[4,256,1024]{2,1,0:T(8,128)}, bf16[3,4,256,1024]{3,2,1,0:T(8,128)(2,1)}, bf16[4,256,1024]{2,1,0:T(8,128)(2,1)}, /*index=5*/s32[]{:T(128)}, s32[]{:T(128)}) while((s32[]{:T(128)}, f32[4]{0:T(128)S(1)}, f32[4,256,1024]{2,1,0:T(8,128)}, bf16[3,4,256,1024]{3,2,1,0:T(8,128)(2,1)}, ...), condition=%wide.region_1.2_spmd.clone, body=%wide.region_0.1_spmd.clone.sunk | while | flops 4299161600 | bytes 39847060 | solution.py:26
  54.3 6.5 %fusion.28 = f32[4,256,4,256]{3,1,2,0:T(8,128)} fusion(bf16[4,256,1024]{2,1,0:T(8,128)(2,1)} %get-tuple-element.109, bf16[3,4,256,1024]{3,2,1,0:T(8,128)(2,1)} %get-tuple-element.108, s32[]{:T(128)} %get-tuple-element.98), kind=kOutput, calls=%fused_computation.4.clone.1 | convolution fusion | flops 2147483648 | bytes 8389120 | tf_op jit(solution)/shard_map/while/body/eval_jaxpr/gip,wjp->wgij/dot_general | solution.py:19
  60.9 5.2 %copy.14 = f32[4,4,256,256]{2,3,0,1:T(8,128)} copy(f32[4,4,256,256]{3,2,0,1:T(8,128)} %bitcast.49) | data formatting | bytes 8388608 | tf_op jit(solution)/shard_map/while
  66.1 4.1 %fusion.29 = f32[4]{0:T(128)S(1)} fusion(f32[4,4,256,256]{2,3,0,1:T(8,128)} %copy.14, f32[4,256,4,256]{3,1,2,0:T(8,128)} %fusion.28), kind=kLoop, calls=%fused_computation.2.clone.1 | loop fusion | flops 2097148 | bytes 8388624 | tf_op jit(solution)/shard_map/while/body/eval_jaxpr/wgij,wgji->w/dot_general | solution.py:20
  70.2 7.2 %bitcast_add_fusion.2 = f32[4,256,1024]{2,1,0:T(8,128)} fusion(f32[4,256,1024]{2,1,0:T(8,128)} %get-tuple-element.100, pred[]{:T(512)S(6)} %compare.3, bf16[3,4,256,1024]{3,2,1,0:T(8,128)(2,1)} %get-tuple-element.108, s32[]{:T(128)} %get-tuple-element.98, f32[4,256,4,256]{3,1,2,0:T(8,128)} %fusion.28), kind=kOutput, calls=%fused_computation.clone.1 | convolution fusion | flops 2149580800 | bytes 14680577 | tf_op jit(solution)/shard_map/while/body/eval_jaxpr/wgki,gip->wkp/dot_general | solution.py:22
  77.4 6.5 %fusion.28 = f32[4,256,4,256]{3,1,2,0:T(8,128)} fusion(bf16[4,256,1024]{2,1,0:T(8,128)(2,1)} %get-tuple-element.109, bf16[3,4,256,1024]{3,2,1,0:T(8,128)(2,1)} %get-tuple-element.108, s32[]{:T(128)} %get-tuple-element.98), kind=kOutput, calls=%fused_computation.4.clone.1 | convolution fusion | flops 2147483648 | bytes 8389120 | tf_op jit(solution)/shard_map/while/body/eval_jaxpr/gip,wjp->wgij/dot_general | solution.py:19
  83.9 5.2 %copy.14 = f32[4,4,256,256]{2,3,0,1:T(8,128)} copy(f32[4,4,256,256]{3,2,0,1:T(8,128)} %bitcast.49) | data formatting | bytes 8388608 | tf_op jit(solution)/shard_map/while
  89.2 4.1 %fusion.29 = f32[4]{0:T(128)S(1)} fusion(f32[4,4,256,256]{2,3,0,1:T(8,128)} %copy.14, f32[4,256,4,256]{3,1,2,0:T(8,128)} %fusion.28), kind=kLoop, calls=%fused_computation.2.clone.1 | loop fusion | flops 2097148 | bytes 8388624 | tf_op jit(solution)/shard_map/while/body/eval_jaxpr/wgij,wgji->w/dot_general | solution.py:20
  93.3 8.4 %bitcast_add_fusion.2 = f32[4,256,1024]{2,1,0:T(8,128)} fusion(f32[4,256,1024]{2,1,0:T(8,128)} %get-tuple-element.100, pred[]{:T(512)S(6)} %compare.3, bf16[3,4,256,1024]{3,2,1,0:T(8,128)(2,1)} %get-tuple-element.108, s32[]{:T(128)} %get-tuple-element.98, f32[4,256,4,256]{3,1,2,0:T(8,128)} %fusion.28), kind=kOutput, calls=%fused_computation.clone.1 | convolution fusion | flops 2149580800 | bytes 14680577 | tf_op jit(solution)/shard_map/while/body/eval_jaxpr/wgki,gip->wkp/dot_general | solution.py:22
  101.6 6.5 %fusion.28 = f32[4,256,4,256]{3,1,2,0:T(8,128)} fusion(bf16[4,256,1024]{2,1,0:T(8,128)(2,1)} %get-tuple-element.109, bf16[3,4,256,1024]{3,2,1,0:T(8,128)(2,1)} %get-tuple-element.108, s32[]{:T(128)} %get-tuple-element.98), kind=kOutput, calls=%fused_computation.4.clone.1 | convolution fusion | flops 2147483648 | bytes 8389120 | tf_op jit(solution)/shard_map/while/body/eval_jaxpr/gip,wjp->wgij/dot_general | solution.py:19
  108.2 5.2 %copy.14 = f32[4,4,256,256]{2,3,0,1:T(8,128)} copy(f32[4,4,256,256]{3,2,0,1:T(8,128)} %bitcast.49) | data formatting | bytes 8388608 | tf_op jit(solution)/shard_map/while
  113.4 4.1 %fusion.29 = f32[4]{0:T(128)S(1)} fusion(f32[4,4,256,256]{2,3,0,1:T(8,128)} %copy.14, f32[4,256,4,256]{3,1,2,0:T(8,128)} %fusion.28), kind=kLoop, calls=%fused_computation.2.clone.1 | loop fusion | flops 2097148 | bytes 8388624 | tf_op jit(solution)/shard_map/while/body/eval_jaxpr/wgij,wgji->w/dot_general | solution.py:20
  117.5 8.4 %bitcast_add_fusion.2 = f32[4,256,1024]{2,1,0:T(8,128)} fusion(f32[4,256,1024]{2,1,0:T(8,128)} %get-tuple-element.100, pred[]{:T(512)S(6)} %compare.3, bf16[3,4,256,1024]{3,2,1,0:T(8,128)(2,1)} %get-tuple-element.108, s32[]{:T(128)} %get-tuple-element.98, f32[4,256,4,256]{3,1,2,0:T(8,128)} %fusion.28), kind=kOutput, calls=%fused_computation.clone.1 | convolution fusion | flops 2149580800 | bytes 14680577 | tf_op jit(solution)/shard_map/while/body/eval_jaxpr/wgki,gip->wkp/dot_general | solution.py:22
  125.9 0.0 copy-start
  125.9 0.0 reduce-scatter.2.cloned.1.call-update
  125.9 0.6 copy-done
  126.5 31.5 %psum.7 = f32[4]{0:T(128)S(1)} all-reduce(f32[4]{0:T(128)S(1)} %get-tuple-element.30), channel_id=1, replica_groups=mesh['groups'=2,'chol'=16] {'chol'}, use_global_device_ids=true, to_apply=%region_2.3 | all-reduce | flops 4 | bytes 32 | tf_op jit(solution)/shard_map/psum | solution.py:27
  158.1 0.5 broadcast_multiply_fusion.2
  158.6 38.7 %reduce-scatter.2.cloned.1.call-done = f32[4,16,1024]{2,1,0:T(8,128)} async-done(((f32[4,256,1024]{2,1,0:T(8,128)}), f32[4,16,1024]{2,1,0:T(8,128)}) %reduce-scatter.2.cloned.1.call-update) | async-done | bytes 262160 | tf_op jit(solution)/shard_map/reduce_scatter | solution.py:28
  197.3 1.7 broadcast_multiply_fusion
  (6 shorter events, 0.0 us)
Async XLA Ops:
  7.2 47.2 %all-gather.2.cloned.1.call-start = ((), (), s32[]{:S(2)}) async-start(), calls=%async_computation.1 | async-start | bytes 2228224 | tf_op jit(solution)/shard_map/all_gather | solution.py:13
  7.9 189.4 %reduce-scatter.2.cloned.1.call-start = ((), (), s32[]{:S(2)}) async-start(), calls=%async_computation.2 | async-start | bytes 4456448 | tf_op jit(solution)/shard_map/reduce_scatter | solution.py:28
  125.9 0.7 copy-start
Sparse Core Ops, SparseCore 0:
  10.2 44.1 all-gather.1
  126.0 71.2 reduce-scatter.1
where the time goes:
time: 206 us
  waiting for transfers between devices  85.8 us (42%)
  matrix products  43.5 us (21%)
  blocking collectives  31.5 us (15%)
  local copies, waits for them, and re-layouts  16.4 us (8%)
  other arithmetic  14.6 us (7%)
  between operations  14.1 us (7%)
    all_gather x1, waiting for transfers between devices, per_device(): full_green = lax.all_gather(green, 'chol', axis=1, tiled=True)  46.4 us
    reduce_scatter x1, waiting for transfers between devices, per_device(): lax.psum_scatter(grad_part, 'chol', scatter_dimension=1, tiled=True)  38.7 us
    psum x1, blocking collectives, per_device(): energy_sum = lax.psum(energy_part, 'chol')  31.5 us
    dot_general x3, matrix products, step(): jnp.einsum('wgki,gip->wkp', thalf, lblock, preferred_element_type=jnp.flo...  23.9 us
    dot_general x3, matrix products, step(): jnp.einsum('gip,wjp->wgij', lblock, full_green, preferred_element_type=jn...  19.5 us
    while x3, local copies, waits for them, and re-layouts  15.7 us
    dot_general x3, other arithmetic, step(): pairs = jnp.einsum('wgij,wgji->w', tmat, tmat)  12.3 us
  transfers between devices with their start and end apart: 2, of which 2 were waited for; matrix products, arithmetic and copies ran while one was open for 0% of the time, Pallas kernels for 0%

commit v1 on v0

--- a/solution.py
+++ b/solution.py
@@ -1,17 +1,291 @@
+import functools
+
 import jax
 import jax.numpy as jnp
 from jax import lax
+from jax.experimental import pallas as pl
+from jax.experimental.pallas import tpu as pltpu
 from jax.sharding import PartitionSpec as P
 
-
-def per_device(green, chol_vecs, cotangent):
+CORES = 2
+COLUMNS = 2
+
+
+def exchange_kernel(
+    scale,
+    cot_ref, green_ref, chol_ref,
+    energy_ref, grad_ref,
+    vecs, full, half, partial, pair, ysend, yrecv, kept, zsend, zrecv, final,
+    eparts, eyparts, ezparts, erecv_c, erecv_y, erecv_z,
+    load_sem, gz_send, gz_recv, gy_send, gy_recv, gc_send, gc_recv,
+    rc_send, rc_recv, ry_send, ry_recv, rz_send, rz_recv,
+    ec_sem, ey_sem, ez_send, ez_recv,
+):
+    walkers, rows, basis = green_ref.shape
+    count, occupied, _ = chol_ref.shape
+    planes = full.shape[1]
+    bf16, f32 = jnp.bfloat16, jnp.float32
+
+    me = lax.axis_index("chol")
+    c = lax.rem(me, CORES)
+    y = lax.rem(me // CORES, COLUMNS)
+    z = me // (CORES * COLUMNS)
+
+    def device(zz, yy, cc):
+        return {"chol": (zz * COLUMNS + yy) * CORES + cc}
+
+    plane = [lax.rem(z + k, planes) for k in range(planes)]
+    source = [lax.rem(z - k + planes, planes) for k in range(planes)]
+    over_z = [device(plane[k], y, c) for k in range(1, planes)]
+    over_y = device(z, 1 - y, c)
+    over_c = device(z, y, 1 - c)
+
+    loads = load_sem.shape[0]
+    per = count // loads
+    for i in range(loads):
+        pltpu.make_async_copy(
+            chol_ref.at[pl.ds(i * per, per)], vecs.at[pl.ds(i * per, per)], load_sem.at[i]
+        ).start()
+    for w in range(walkers):
+        full[w, z, y, c] = green_ref[w]
+
+    barrier = pltpu.get_barrier_semaphore()
+    for peer in over_z + [over_y, over_c]:
+        pl.semaphore_signal(barrier, inc=1, device_id=peer, device_id_type=pl.DeviceIdType.MESH)
+    pl.semaphore_wait(barrier, planes + 1)
+
+    sent = []
+
+    def send(src, dst, send_sem, recv_sem, peer):
+        copy = pltpu.make_async_remote_copy(
+            src_ref=src, dst_ref=dst, send_sem=send_sem, recv_sem=recv_sem,
+            device_id=peer, device_id_type=pl.DeviceIdType.MESH,
+        )
+        copy.start()
+        sent.append(copy)
+        return copy
+
+    gz = [[None] * planes for _ in range(walkers)]
+    gy = [[None] * planes for _ in range(walkers)]
+    gc = [[None] * COLUMNS for _ in range(walkers)]
+
+    def pass_y(w, k):
+        block = full.at[w, source[k], y, c]
+        gy[w][k] = send(block, block, gy_send.at[w, k], gy_recv.at[w, k], over_y)
+
+    for w in range(walkers):
+        block = full.at[w, z, y, c]
+        for k in range(planes - 1, 0, -1):
+            gz[w][k] = send(block, block, gz_send.at[w, k - 1], gz_recv.at[w, k - 1], over_z[k - 1])
+        pass_y(w, 0)
+
+    def gather_z(w):
+        for k in range(1, planes):
+            gz[w][k].wait_recv()
+            pass_y(w, k)
+        own = full.at[w, :, y, c]
+        gc[w][0] = send(own, own, gc_send.at[w, 0], gc_recv.at[w, 0], over_c)
+
+    def gather_y(w):
+        for k in range(planes):
+            gy[w][k].wait_recv()
+        other = full.at[w, :, 1 - y, c]
+        gc[w][1] = send(other, other, gc_send.at[w, 1], gc_recv.at[w, 1], over_c)
+
+    def gather_c(w):
+        for k in range(COLUMNS):
+            gc[w][k].wait_recv()
+
+    def make_tmat(w):
+        eparts[w] = jnp.zeros_like(eparts[w])
+
+        @pl.loop(0, loads)
+        def _(i):
+            first = i * per
+            if w == 0:
+                pltpu.make_async_copy(
+                    chol_ref.at[pl.ds(first, per)], vecs.at[pl.ds(first, per)], load_sem.at[i]
+                ).wait()
+            left = vecs[pl.ds(first, per)].reshape(per * occupied, basis)
+            right = full[w].reshape(occupied, basis)
+            tmat = lax.dot_general(left, right, (((1,), (1,)), ((), ())), preferred_element_type=f32)
+            total = jnp.zeros(eparts.shape[1:], f32)
+            for j in range(per):
+                one = tmat[j * occupied:(j + 1) * occupied]
+                at = pl.multiple_of((first + j) * occupied, occupied)
+                half[:, pl.ds(at, occupied)] = one.astype(bf16)
+                pairs = one * one.T
+                folded = pairs.reshape(occupied // 8, 8, occupied).sum(axis=0)
+                for lane in range(0, occupied, 128):
+                    total += folded[:, lane:lane + 128]
+            eparts[w] += total
+
+    chunk = 256 if basis % 256 == 0 else 128
+
+    def make_grad(w):
+        @pl.loop(0, basis // chunk)
+        def _(i):
+            at = pl.multiple_of(i * chunk, chunk)
+            right = vecs[:, :, pl.ds(at, chunk)].reshape(count * occupied, chunk)
+            part = jnp.dot(half[...], right, preferred_element_type=f32)
+            for zz in range(planes):
+                for yy in range(COLUMNS):
+                    for cc in range(CORES):
+                        row = ((zz * COLUMNS + yy) * CORES + cc) * rows
+                        partial[w, cc, yy, zz, :, pl.ds(at, chunk)] = part[row:row + rows]
+
+    rc, ry = [None] * walkers, [None] * walkers
+    rz = [[None] * planes for _ in range(walkers)]
+
+    def reduce_c(w):
+        rc[w] = send(partial.at[w, 1 - c], pair.at[w], rc_send.at[w], rc_recv.at[w], over_c)
+
+    def reduce_y(w):
+        rc[w].wait_recv()
+        ysend[w] = (partial[w, c, 1 - y] + pair[w, 1 - y]).astype(bf16)
+        ry[w] = send(ysend.at[w], yrecv.at[w], ry_send.at[w], ry_recv.at[w], over_y)
+        kept[w] = partial[w, c, y] + pair[w, y]
+
+    def reduce_z(w):
+        ry[w].wait_recv()
+        zsend[w] = (kept[w] + yrecv[w].astype(f32)).astype(bf16)
+        for k in range(planes - 1, 0, -1):
+            rz[w][k] = send(
+                zsend.at[w, plane[k]], zrecv.at[w, k - 1], rz_send.at[w, k - 1], rz_recv.at[w, k - 1], over_z[k - 1]
+            )
+        final[w] = kept[w, z] + yrecv[w, z].astype(f32)
+
+    def finish(w):
+        total = final[w]
+        for k in range(1, planes):
+            rz[w][k].wait_recv()
+            total += zrecv[w, k - 1].astype(f32)
+        grad_ref[w] = (-scale * cot_ref[w]) * total
+
+    last = walkers - 1
+    gather_z(0)
+    if walkers > 1:
+        gather_z(1)
+    gather_y(0)
+    gather_c(0)
+    for w in range(walkers):
+        make_tmat(w)
+        if w > 0:
+            reduce_y(w - 1)
+        if w > 1:
+            finish(w - 2)
+        if w == last:
+            ec = send(eparts, erecv_c, ec_sem.at[0], ec_sem.at[1], over_c)
+        if w + 2 < walkers:
+            gather_z(w + 2)
+        if w + 1 < walkers:
+            gather_y(w + 1)
+        make_grad(w)
+        reduce_c(w)
+        if w > 0:
+            reduce_z(w - 1)
+        if w + 1 < walkers:
+            gather_c(w + 1)
+    ec.wait_recv()
+    eyparts[...] = eparts[...] + erecv_c[...]
+    ey = send(eyparts, erecv_y, ey_sem.at[0], ey_sem.at[1], over_y)
+    reduce_y(last)
+    if last > 0:
+        finish(last - 1)
+    ey.wait_recv()
+    ezparts[...] = eyparts[...] + erecv_y[...]
+    ez = [
+        send(ezparts, erecv_z.at[k - 1], ez_send.at[k - 1], ez_recv.at[k - 1], over_z[k - 1])
+        for k in range(1, planes)
+    ]
+    reduce_z(last)
+    esum = ezparts[...]
+    for k in range(1, planes):
+        ez[k - 1].wait_recv()
+        esum += erecv_z[k - 1]
+    for w in range(walkers):
+        energy_ref[w] = -0.5 * scale * jnp.sum(esum[w])
+    finish(last)
+    for copy in sent:
+        copy.wait_send()
+
+
+def per_device_kernel(green, chol_vecs, cotangent):
+    walkers, rows, basis = green.shape
+    count, occupied, _ = chol_vecs.shape
+    devices = lax.axis_size("chol")
+    planes = devices // (CORES * COLUMNS)
+    scale = 1.0 / (occupied * count * devices)
+    per = max(i for i in (1, 2, 3) if count % i == 0)
+    loads = count // per
+    bf16, f32 = jnp.bfloat16, jnp.float32
+    block = (rows, basis)
+    dma = pltpu.SemaphoreType.DMA
+    others = planes - 1
+    estack = (walkers, 8, 128)
+    energy, grad_green = pl.pallas_call(
+        functools.partial(exchange_kernel, scale),
+        out_shape=(
+            jax.ShapeDtypeStruct((walkers,), f32),
+            jax.ShapeDtypeStruct((walkers,) + block, f32),
+        ),
+        in_specs=[
+            pl.BlockSpec(memory_space=pltpu.SMEM),
+            pl.BlockSpec(memory_space=pltpu.VMEM),
+            pl.BlockSpec(memory_space=pl.ANY),
+        ],
+        out_specs=(
+            pl.BlockSpec(memory_space=pltpu.SMEM),
+            pl.BlockSpec(memory_space=pltpu.VMEM),
+        ),
+        scratch_shapes=[
+            pltpu.VMEM((count, occupied, basis), bf16),
+            pltpu.VMEM((walkers, planes, COLUMNS, CORES) + block, bf16),
+            pltpu.VMEM((occupied, count * occupied), bf16),
+            pltpu.VMEM((walkers, CORES, COLUMNS, planes) + block, f32),
+            pltpu.VMEM((walkers, COLUMNS, planes) + block, f32),
+            pltpu.VMEM((walkers, planes) + block, bf16),
+            pltpu.VMEM((walkers, planes) + block, bf16),
+            pltpu.VMEM((walkers, planes) + block, f32),
+            pltpu.VMEM((walkers, planes) + block, bf16),
+            pltpu.VMEM((walkers, others) + block, bf16),
+            pltpu.VMEM((walkers,) + block, f32),
+            pltpu.VMEM(estack, f32),
+            pltpu.VMEM(estack, f32),
+            pltpu.VMEM(estack, f32),
+            pltpu.VMEM(estack, f32),
+            pltpu.VMEM(estack, f32),
+            pltpu.VMEM((others,) + estack, f32),
+            dma((loads,)),
+            dma((walkers, others)), dma((walkers, others)),
+            dma((walkers, planes)), dma((walkers, planes)),
+            dma((walkers, COLUMNS)), dma((walkers, COLUMNS)),
+            dma((walkers,)), dma((walkers,)),
+            dma((walkers,)), dma((walkers,)),
+            dma((walkers, others)), dma((walkers, others)),
+            dma((2,)), dma((2,)),
+            dma((others,)), dma((others,)),
+        ],
+        compiler_params=pltpu.CompilerParams(
+            collective_id=0, has_side_effects=True, vmem_limit_bytes=48 * 1024 * 1024
+        ),
+        cost_estimate=pl.CostEstimate(
+            flops=4 * walkers * count * occupied * occupied * basis,
+            bytes_accessed=2 * chol_vecs.size,
+            transcendentals=0,
+        ),
+    )(cotangent, green, chol_vecs)
+    return (energy, grad_green)
+
+
+def per_device_plain(green, chol_vecs, cotangent):
     count = chol_vecs.shape[0]
     walkers = green.shape[0]
     occupied = chol_vecs.shape[1]
     basis = chol_vecs.shape[2]
     scale = 1.0 / (occupied * count * lax.axis_size("chol"))
     full_green = lax.all_gather(green, "chol", axis=1, tiled=True)
-    per_block = 4
+    per_block = 4 if count % 4 == 0 else 1
     blocks = chol_vecs.reshape(count // per_block, per_block, occupied, basis)
 
     def step(carry, lblock):
@@ -29,6 +303,19 @@
     energy = -0.5 * scale * energy_sum
     grad_green = -scale * cotangent[:, None, None] * own_rows
     return (energy, grad_green)
+
+
+def per_device(green, chol_vecs, cotangent):
+    devices = lax.axis_size("chol")
+    fits = (
+        devices % (CORES * COLUMNS) == 0
+        and devices > CORES * COLUMNS
+        and green.shape[1] % 16 == 0
+        and chol_vecs.shape[1] % 128 == 0
+        and chol_vecs.shape[2] % 128 == 0
+    )
+    run = per_device_kernel if fits else per_device_plain
+    return run(green, chol_vecs, cotangent)
 
 
 def solution(mesh):

time: 206 us -> 61.4 us (0.30)
  waiting for transfers between devices: 85.8 us -> 0 us
  Pallas kernels: 0 us -> 57.8 us
  matrix products: 43.5 us -> 0 us
  blocking collectives: 31.5 us -> 0 us
  other arithmetic: 14.6 us -> 0 us
  local copies, waits for them, and re-layouts: 16.4 us -> 2.77 us
  between operations: 14.1 us -> 0.65 us
    pallas_call x0 -> x1, Pallas kernels: none -> 57.8 us  [per_device_kernel(): pl.pallas_call(functools.partial(exchange_kernel, scale), out_shape=(jax....]
    all_gather x1 -> x0, waiting for transfers between devices: 46.4 us -> none  [per_device(): full_green = lax.all_gather(green, 'chol', axis=1, tiled=True)]
    dot_general x6 -> x0, matrix products: 43.5 us -> none  [the longest x3 23.9 us: step(): jnp.einsum('wgki,gip->wkp', thalf, lblock, preferred_element_type=jnp.flo...]
    reduce_scatter x1 -> x0, waiting for transfers between devices: 38.7 us -> none  [per_device(): lax.psum_scatter(grad_part, 'chol', scatter_dimension=1, tiled=True)]
    psum x1 -> x0, blocking collectives: 31.5 us -> none  [per_device(): energy_sum = lax.psum(energy_part, 'chol')]
    while x3 -> x0, local copies, waits for them, and re-layouts: 15.7 us -> none
    dot_general x3 -> x0, other arithmetic: 12.3 us -> none  [step(): pairs = jnp.einsum('wgij,wgji->w', tmat, tmat)]
    mul x3 -> x0, other arithmetic: 2.26 us -> none  [the longest x2 1.74 us: per_device(): grad_green = -scale * cotangent[:, None, None] * own_rows]
  transfers between devices with their start and end apart: 2 -> 0, of which waited for: 2 -> 0; matrix products, arithmetic and copies ran while one was open for 0% -> 0% of each run, Pallas kernels for 0% -> 0%
where the time goes in v1:
time: 61.4 us; the launch traced here: 61.3 us
  Pallas kernels  57.8 us (94%)
  local copies, waits for them, and re-layouts  2.77 us (5%)
  between operations  0.65 us (1%)
    pallas_call x1, Pallas kernels, per_device_kernel(): pl.pallas_call(functools.partial(exchange_kernel, scale), out_shape=(jax....  57.8 us
    unnamed x6, local copies, waits for them, and re-layouts  2.77 us

profile of v1, /device:TPU:0, one launch (start us, length us, event | category | flops | bytes accessed | tf_op | source)
XLA Modules:
  0.0 61.3 jit_solution(11289376110022649744)
XLA Ops:
  0.6 0.0 copy-start
  0.6 0.9 %copy-done = bf16[4,16,1024]{2,1,0:T(8,128)(2,1)S(1)} copy-done((bf16[4,16,1024]{2,1,0:T(8,128)(2,1)S(1)}, bf16[4,16,1024]{2,1,0:T(8,128)(2,1)}, u32[]{:S(2)}) %copy-start) | copy-done | bytes 131096
  1.5 0.0 copy-start.1
  1.5 0.7 %copy-done.1 = f32[4]{0:T(128)S(1)} copy-done((f32[4]{0:T(128)S(1)}, f32[4]{0:T(128)}, u32[]{:S(2)}) %copy-start.1) | copy-done | bytes 40
  2.2 57.8 %shard_map.50 = (f32[4]{0:T(128)S(1)}, f32[4,16,1024]{2,1,0:T(8,128)S(1)}) custom-call(f32[4]{0:T(128)S(1)} %copy-done.1, bf16[4,16,1024]{2,1,0:T(8,128)(2,1)S(1)} %copy-done, bf16[12,256,1024]{2,1,0:T(8,128)(2,1)} %chol_ref.1), custom_call_target="tpu_custom_call" | custom-call | flops 12884901888 | bytes 6291456 | tf_op jit(solution)/shard_map/pallas_call | solution.py:226
  60.0 0.5 copy.7
  60.5 0.7 %copy.8 = f32[4,16,1024]{2,1,0:T(8,128)} copy(f32[4,16,1024]{2,1,0:T(8,128)S(1)} %get-tuple-element.5) | data formatting | bytes 524288
Async XLA Ops:
  0.6 0.9 %copy-start = (bf16[4,16,1024]{2,1,0:T(8,128)(2,1)S(1)}, bf16[4,16,1024]{2,1,0:T(8,128)(2,1)}, u32[]{:S(2)}) copy-start(bf16[4,16,1024]{2,1,0:T(8,128)(2,1)} %green_ref.1) | copy-start | bytes 393220
  1.5 0.7 %copy-start.1 = (f32[4]{0:T(128)S(1)}, f32[4]{0:T(128)}, u32[]{:S(2)}) copy-start(f32[4]{0:T(128)} %cot_ref.1) | copy-start | bytes 52

commit v2 on v1

--- a/solution.py
+++ b/solution.py
@@ -13,11 +13,11 @@
 
 def exchange_kernel(
     scale,
-    cot_ref, green_ref, chol_ref,
+    green_ref, chol_ref,
     energy_ref, grad_ref,
     vecs, full, half, partial, pair, ysend, yrecv, kept, zsend, zrecv, final,
     eparts, eyparts, ezparts, erecv_c, erecv_y, erecv_z,
-    load_sem, gz_send, gz_recv, gy_send, gy_recv, gc_send, gc_recv,
+    load_sem, own_sem, gz_send, gz_recv, gy_send, gy_recv, gc_send, gc_recv,
     rc_send, rc_recv, ry_send, ry_recv, rz_send, rz_recv,
     ec_sem, ey_sem, ez_send, ez_recv,
 ):
@@ -40,14 +40,15 @@
     over_y = device(z, 1 - y, c)
     over_c = device(z, y, 1 - c)
 
+    own = [pltpu.make_async_copy(green_ref.at[w], full.at[w, z, y, c], own_sem.at[w]) for w in range(walkers)]
+    for copy in own:
+        copy.start()
     loads = load_sem.shape[0]
     per = count // loads
     for i in range(loads):
         pltpu.make_async_copy(
             chol_ref.at[pl.ds(i * per, per)], vecs.at[pl.ds(i * per, per)], load_sem.at[i]
         ).start()
-    for w in range(walkers):
-        full[w, z, y, c] = green_ref[w]
 
     barrier = pltpu.get_barrier_semaphore()
     for peer in over_z + [over_y, over_c]:
@@ -74,6 +75,7 @@
         gy[w][k] = send(block, block, gy_send.at[w, k], gy_recv.at[w, k], over_y)
 
     for w in range(walkers):
+        own[w].wait()
         block = full.at[w, z, y, c]
         for k in range(planes - 1, 0, -1):
             gz[w][k] = send(block, block, gz_send.at[w, k - 1], gz_recv.at[w, k - 1], over_z[k - 1])
@@ -97,8 +99,6 @@
             gc[w][k].wait_recv()
 
     def make_tmat(w):
-        eparts[w] = jnp.zeros_like(eparts[w])
-
         @pl.loop(0, loads)
         def _(i):
             first = i * per
@@ -109,25 +109,25 @@
             left = vecs[pl.ds(first, per)].reshape(per * occupied, basis)
             right = full[w].reshape(occupied, basis)
             tmat = lax.dot_general(left, right, (((1,), (1,)), ((), ())), preferred_element_type=f32)
-            total = jnp.zeros(eparts.shape[1:], f32)
             for j in range(per):
                 one = tmat[j * occupied:(j + 1) * occupied]
                 at = pl.multiple_of((first + j) * occupied, occupied)
                 half[:, pl.ds(at, occupied)] = one.astype(bf16)
-                pairs = one * one.T
-                folded = pairs.reshape(occupied // 8, 8, occupied).sum(axis=0)
-                for lane in range(0, occupied, 128):
-                    total += folded[:, lane:lane + 128]
-            eparts[w] += total
 
     chunk = 256 if basis % 256 == 0 else 128
 
     def make_grad(w):
+        eparts[w] = jnp.zeros_like(eparts[w])
+
         @pl.loop(0, basis // chunk)
         def _(i):
             at = pl.multiple_of(i * chunk, chunk)
             right = vecs[:, :, pl.ds(at, chunk)].reshape(count * occupied, chunk)
             part = jnp.dot(half[...], right, preferred_element_type=f32)
+            green = full[w, :, :, :, :, pl.ds(at, chunk)].reshape(occupied, chunk)
+            folded = (part * green.astype(f32)).reshape(occupied // 8, 8, chunk).sum(axis=0)
+            for lane in range(0, chunk, 128):
+                eparts[w] += folded[:, lane:lane + 128]
             for zz in range(planes):
                 for yy in range(COLUMNS):
                     for cc in range(CORES):
@@ -160,7 +160,7 @@
         for k in range(1, planes):
             rz[w][k].wait_recv()
             total += zrecv[w, k - 1].astype(f32)
-        grad_ref[w] = (-scale * cot_ref[w]) * total
+        grad_ref[w] = -scale * total
 
     last = walkers - 1
     gather_z(0)
@@ -174,13 +174,13 @@
             reduce_y(w - 1)
         if w > 1:
             finish(w - 2)
-        if w == last:
-            ec = send(eparts, erecv_c, ec_sem.at[0], ec_sem.at[1], over_c)
         if w + 2 < walkers:
             gather_z(w + 2)
         if w + 1 < walkers:
             gather_y(w + 1)
         make_grad(w)
+        if w == last:
+            ec = send(eparts, erecv_c, ec_sem.at[0], ec_sem.at[1], over_c)
         reduce_c(w)
         if w > 0:
             reduce_z(w - 1)
@@ -203,8 +203,7 @@
     for k in range(1, planes):
         ez[k - 1].wait_recv()
         esum += erecv_z[k - 1]
-    for w in range(walkers):
-        energy_ref[w] = -0.5 * scale * jnp.sum(esum[w])
+    energy_ref[...] = -0.5 * scale * esum
     finish(last)
     for copy in sent:
         copy.wait_send()
@@ -223,19 +222,18 @@
     dma = pltpu.SemaphoreType.DMA
     others = planes - 1
     estack = (walkers, 8, 128)
-    energy, grad_green = pl.pallas_call(
+    energy_parts, own_rows = pl.pallas_call(
         functools.partial(exchange_kernel, scale),
         out_shape=(
-            jax.ShapeDtypeStruct((walkers,), f32),
+            jax.ShapeDtypeStruct(estack, f32),
             jax.ShapeDtypeStruct((walkers,) + block, f32),
         ),
         in_specs=[
-            pl.BlockSpec(memory_space=pltpu.SMEM),
-            pl.BlockSpec(memory_space=pltpu.VMEM),
+            pl.BlockSpec(memory_space=pl.ANY),
             pl.BlockSpec(memory_space=pl.ANY),
         ],
         out_specs=(
-            pl.BlockSpec(memory_space=pltpu.SMEM),
+            pl.BlockSpec(memory_space=pltpu.VMEM),
             pl.BlockSpec(memory_space=pltpu.VMEM),
         ),
         scratch_shapes=[
@@ -256,7 +254,7 @@
             pltpu.VMEM(estack, f32),
             pltpu.VMEM(estack, f32),
             pltpu.VMEM((others,) + estack, f32),
-            dma((loads,)),
+            dma((loads,)), dma((walkers,)),
             dma((walkers, others)), dma((walkers, others)),
             dma((walkers, planes)), dma((walkers, planes)),
             dma((walkers, COLUMNS)), dma((walkers, COLUMNS)),
@@ -267,14 +265,16 @@
             dma((others,)), dma((others,)),
         ],
         compiler_params=pltpu.CompilerParams(
-            collective_id=0, has_side_effects=True, vmem_limit_bytes=48 * 1024 * 1024
+            collective_id=0, has_side_effects=True, vmem_limit_bytes=60 * 1024 * 1024
         ),
         cost_estimate=pl.CostEstimate(
             flops=4 * walkers * count * occupied * occupied * basis,
             bytes_accessed=2 * chol_vecs.size,
             transcendentals=0,
         ),
-    )(cotangent, green, chol_vecs)
+    )(green, chol_vecs)
+    energy = jnp.sum(energy_parts, axis=(1, 2))
+    grad_green = cotangent[:, None, None] * own_rows
     return (energy, grad_green)
 
 

time: 61.4 us -> 60.6 us (0.987)
  other arithmetic: 0 us -> 3.08 us
  local copies, waits for them, and re-layouts: 2.77 us -> 0.01 us
  Pallas kernels: 57.8 us -> 56.6 us
    unnamed x6 -> x2, local copies, waits for them, and re-layouts: 2.77 us -> 0.01 us
    mul x0 -> x1, other arithmetic: none -> 1.74 us  [per_device_kernel(): grad_green = cotangent[:, None, None] * own_rows]
    reduce_sum x0 -> x1, other arithmetic: none -> 1.34 us  [per_device_kernel(): energy = jnp.sum(energy_parts, axis=(1, 2))]
    pallas_call x1, Pallas kernels: 57.8 us -> 56.6 us  [per_device_kernel(): pl.pallas_call(functools.partial(exchange_kernel, scale), out_shape=(jax....]
where the time goes in v2:
time: 60.6 us; the launch traced here: 60.3 us
  Pallas kernels  56.6 us (93%)
  other arithmetic  3.08 us (5%)
  between operations  0.65 us (1%)
    pallas_call x1, Pallas kernels, per_device_kernel(): pl.pallas_call(functools.partial(exchange_kernel, scale), out_shape=(jax....  56.6 us
    mul x1, other arithmetic, per_device_kernel(): grad_green = cotangent[:, None, None] * own_rows  1.74 us
    reduce_sum x1, other arithmetic, per_device_kernel(): energy = jnp.sum(energy_parts, axis=(1, 2))  1.34 us

profile of v2, /device:TPU:0, one launch (start us, length us, event | category | flops | bytes accessed | tf_op | source)
XLA Modules:
  0.0 60.3 jit_solution(7848704322595508464)
XLA Ops:
  0.6 0.0 copy-start
  0.6 56.6 %shard_map.50 = (f32[4,8,128]{2,1,0:T(8,128)}, f32[4,16,1024]{2,1,0:T(8,128)}) custom-call(bf16[4,16,1024]{2,1,0:T(8,128)(2,1)} %green_ref.1, bf16[12,256,1024]{2,1,0:T(8,128)(2,1)} %chol_ref.1), custom_call_target="tpu_custom_call" | custom-call | flops 12884901888 | bytes 6291456 | tf_op jit(solution)/shard_map/pallas_call | solution.py:225
  57.3 1.3 %reduce_sum.9 = f32[4]{0:T(128)} reduce(f32[4,8,128]{2,1,0:T(8,128)} %get-tuple-element.4, f32[]{:T(128)} %constant.0.clone.1), dimensions={1,2}, to_apply=%region_0.0 | reduce | flops 4092 | bytes 16404 | tf_op jit(solution)/shard_map/reduce_sum | solution.py:276
  58.6 0.0 copy-done
  58.6 1.7 %broadcast_multiply_fusion = f32[4,16,1024]{2,1,0:T(8,128)} fusion(f32[4,16,1024]{2,1,0:T(8,128)} %get-tuple-element.5, f32[4]{0:T(128)S(1)} %copy-done), kind=kLoop, calls=%fused_computation | loop fusion | flops 65536 | bytes 524304 | tf_op jit(solution)/shard_map/mul | solution.py:277
Async XLA Ops:
  0.6 58.0 %copy-start = (f32[4]{0:T(128)S(1)}, f32[4]{0:T(128)}, u32[]{:S(2)}) copy-start(f32[4]{0:T(128)} %param.5) | copy-start | bytes 52

commit v3 on v2

--- a/solution.py
+++ b/solution.py
@@ -74,17 +74,22 @@
         block = full.at[w, source[k], y, c]
         gy[w][k] = send(block, block, gy_send.at[w, k], gy_recv.at[w, k], over_y)
 
-    for w in range(walkers):
+    def offer(w):
         own[w].wait()
         block = full.at[w, z, y, c]
         for k in range(planes - 1, 0, -1):
             gz[w][k] = send(block, block, gz_send.at[w, k - 1], gz_recv.at[w, k - 1], over_z[k - 1])
         pass_y(w, 0)
 
+    for w in range(min(2, walkers)):
+        offer(w)
+
     def gather_z(w):
         for k in range(1, planes):
             gz[w][k].wait_recv()
             pass_y(w, k)
+        if w + 2 < walkers:
+            offer(w + 2)
         own = full.at[w, :, y, c]
         gc[w][0] = send(own, own, gc_send.at[w, 0], gc_recv.at[w, 0], over_c)
 

time: 60.6 us -> 60.6 us (level)
  no operation moved by 1% of the time
where the time goes in v3:
time: 60.6 us; the launch traced here: 60.3 us
  Pallas kernels  56.6 us (93%)
  other arithmetic  3.08 us (5%)
  between operations  0.65 us (1%)
    pallas_call x1, Pallas kernels, per_device_kernel(): pl.pallas_call(functools.partial(exchange_kernel, scale), out_shape=(jax....  56.6 us
    mul x1, other arithmetic, per_device_kernel(): grad_green = cotangent[:, None, None] * own_rows  1.74 us
    reduce_sum x1, other arithmetic, per_device_kernel(): energy = jnp.sum(energy_parts, axis=(1, 2))  1.34 us

profile of v3, /device:TPU:0, one launch (start us, length us, event | category | flops | bytes accessed | tf_op | source)
XLA Modules:
  0.0 60.3 jit_solution(7788738072599071282)
XLA Ops:
  0.6 0.0 copy-start
  0.6 56.6 %shard_map.50 = (f32[4,8,128]{2,1,0:T(8,128)}, f32[4,16,1024]{2,1,0:T(8,128)}) custom-call(bf16[4,16,1024]{2,1,0:T(8,128)(2,1)} %green_ref.1, bf16[12,256,1024]{2,1,0:T(8,128)(2,1)} %chol_ref.1), custom_call_target="tpu_custom_call" | custom-call | flops 12884901888 | bytes 6291456 | tf_op jit(solution)/shard_map/pallas_call | solution.py:230
  57.3 1.3 %reduce_sum.9 = f32[4]{0:T(128)} reduce(f32[4,8,128]{2,1,0:T(8,128)} %get-tuple-element.4, f32[]{:T(128)} %constant.0.clone.1), dimensions={1,2}, to_apply=%region_0.0 | reduce | flops 4092 | bytes 16404 | tf_op jit(solution)/shard_map/reduce_sum | solution.py:281
  58.6 0.0 copy-done
  58.6 1.7 %broadcast_multiply_fusion = f32[4,16,1024]{2,1,0:T(8,128)} fusion(f32[4,16,1024]{2,1,0:T(8,128)} %get-tuple-element.5, f32[4]{0:T(128)S(1)} %copy-done), kind=kLoop, calls=%fused_computation | loop fusion | flops 65536 | bytes 524304 | tf_op jit(solution)/shard_map/mul | solution.py:282
Async XLA Ops:
  0.6 58.0 %copy-start = (f32[4]{0:T(128)S(1)}, f32[4]{0:T(128)}, u32[]{:S(2)}) copy-start(f32[4]{0:T(128)} %param.5) | copy-start | bytes 52

commit v4 on v2

--- a/solution.py
+++ b/solution.py
@@ -45,79 +45,85 @@
         copy.start()
     loads = load_sem.shape[0]
     per = count // loads
+
+    def load(i):
+        return pltpu.make_async_copy(
+            chol_ref.at[pl.ds(i * per, per)], vecs.at[pl.ds(i * per, per)], load_sem.at[i]
+        )
+
     for i in range(loads):
-        pltpu.make_async_copy(
-            chol_ref.at[pl.ds(i * per, per)], vecs.at[pl.ds(i * per, per)], load_sem.at[i]
-        ).start()
+        load(i).start()
 
     barrier = pltpu.get_barrier_semaphore()
     for peer in over_z + [over_y, over_c]:
         pl.semaphore_signal(barrier, inc=1, device_id=peer, device_id_type=pl.DeviceIdType.MESH)
     pl.semaphore_wait(barrier, planes + 1)
 
-    sent = []
-
-    def send(src, dst, send_sem, recv_sem, peer):
-        copy = pltpu.make_async_remote_copy(
+    def remote(src, dst, send_sem, recv_sem, peer):
+        return pltpu.make_async_remote_copy(
             src_ref=src, dst_ref=dst, send_sem=send_sem, recv_sem=recv_sem,
             device_id=peer, device_id_type=pl.DeviceIdType.MESH,
         )
-        copy.start()
-        sent.append(copy)
-        return copy
-
-    gz = [[None] * planes for _ in range(walkers)]
-    gy = [[None] * planes for _ in range(walkers)]
-    gc = [[None] * COLUMNS for _ in range(walkers)]
-
-    def pass_y(w, k):
+
+    def copy_gz(w, k):
+        block = full.at[w, z, y, c]
+        return remote(block, block, gz_send.at[w, k - 1], gz_recv.at[w, k - 1], over_z[k - 1])
+
+    def copy_gy(w, k):
         block = full.at[w, source[k], y, c]
-        gy[w][k] = send(block, block, gy_send.at[w, k], gy_recv.at[w, k], over_y)
-
-    for w in range(walkers):
-        own[w].wait()
-        block = full.at[w, z, y, c]
+        return remote(block, block, gy_send.at[w, k], gy_recv.at[w, k], over_y)
+
+    def copy_gc(w, k):
+        column = full.at[w, :, y if k == 0 else 1 - y, c]
+        return remote(column, column, gc_send.at[w, k], gc_recv.at[w, k], over_c)
+
+    def copy_rc(w):
+        return remote(partial.at[w, 1 - c], pair.at[w], rc_send.at[w], rc_recv.at[w], over_c)
+
+    def copy_ry(w):
+        return remote(ysend.at[w], yrecv.at[w], ry_send.at[w], ry_recv.at[w], over_y)
+
+    def copy_rz(w, k):
+        return remote(
+            zsend.at[w, plane[k]], zrecv.at[w, k - 1], rz_send.at[w, k - 1], rz_recv.at[w, k - 1], over_z[k - 1]
+        )
+
+    def offer(w):
+        pltpu.make_async_copy(green_ref.at[w], full.at[w, z, y, c], own_sem.at[w]).wait()
         for k in range(planes - 1, 0, -1):
-            gz[w][k] = send(block, block, gz_send.at[w, k - 1], gz_recv.at[w, k - 1], over_z[k - 1])
-        pass_y(w, 0)
+            copy_gz(w, k).start()
+        copy_gy(w, 0).start()
 
     def gather_z(w):
         for k in range(1, planes):
-            gz[w][k].wait_recv()
-            pass_y(w, k)
-        own = full.at[w, :, y, c]
-        gc[w][0] = send(own, own, gc_send.at[w, 0], gc_recv.at[w, 0], over_c)
+            copy_gz(w, k).wait_recv()
+            copy_gy(w, k).start()
+        copy_gc(w, 0).start()
 
     def gather_y(w):
         for k in range(planes):
-            gy[w][k].wait_recv()
-        other = full.at[w, :, 1 - y, c]
-        gc[w][1] = send(other, other, gc_send.at[w, 1], gc_recv.at[w, 1], over_c)
+            copy_gy(w, k).wait_recv()
+        copy_gc(w, 1).start()
 
     def gather_c(w):
         for k in range(COLUMNS):
-            gc[w][k].wait_recv()
+            copy_gc(w, k).wait_recv()
 
     def make_tmat(w):
         @pl.loop(0, loads)
         def _(i):
             first = i * per
-            if w == 0:
-                pltpu.make_async_copy(
-                    chol_ref.at[pl.ds(first, per)], vecs.at[pl.ds(first, per)], load_sem.at[i]
-                ).wait()
             left = vecs[pl.ds(first, per)].reshape(per * occupied, basis)
             right = full[w].reshape(occupied, basis)
             tmat = lax.dot_general(left, right, (((1,), (1,)), ((), ())), preferred_element_type=f32)
             for j in range(per):
-                one = tmat[j * occupied:(j + 1) * occupied]
                 at = pl.multiple_of((first + j) * occupied, occupied)
-                half[:, pl.ds(at, occupied)] = one.astype(bf16)
+                half[:, pl.ds(at, occupied)] = tmat[j * occupied:(j + 1) * occupied].astype(bf16)
 
     chunk = 256 if basis % 256 == 0 else 128
 
     def make_grad(w):
-        eparts[w] = jnp.zeros_like(eparts[w])
+        eparts[w] = jnp.zeros(eparts.shape[1:], f32)
 
         @pl.loop(0, basis // chunk)
         def _(i):
@@ -134,79 +140,107 @@
                         row = ((zz * COLUMNS + yy) * CORES + cc) * rows
                         partial[w, cc, yy, zz, :, pl.ds(at, chunk)] = part[row:row + rows]
 
-    rc, ry = [None] * walkers, [None] * walkers
-    rz = [[None] * planes for _ in range(walkers)]
-
-    def reduce_c(w):
-        rc[w] = send(partial.at[w, 1 - c], pair.at[w], rc_send.at[w], rc_recv.at[w], over_c)
-
     def reduce_y(w):
-        rc[w].wait_recv()
+        copy_rc(w).wait_recv()
         ysend[w] = (partial[w, c, 1 - y] + pair[w, 1 - y]).astype(bf16)
-        ry[w] = send(ysend.at[w], yrecv.at[w], ry_send.at[w], ry_recv.at[w], over_y)
+        copy_ry(w).start()
         kept[w] = partial[w, c, y] + pair[w, y]
 
     def reduce_z(w):
-        ry[w].wait_recv()
+        copy_ry(w).wait_recv()
         zsend[w] = (kept[w] + yrecv[w].astype(f32)).astype(bf16)
         for k in range(planes - 1, 0, -1):
-            rz[w][k] = send(
-                zsend.at[w, plane[k]], zrecv.at[w, k - 1], rz_send.at[w, k - 1], rz_recv.at[w, k - 1], over_z[k - 1]
-            )
+            copy_rz(w, k).start()
         final[w] = kept[w, z] + yrecv[w, z].astype(f32)
 
     def finish(w):
         total = final[w]
         for k in range(1, planes):
-            rz[w][k].wait_recv()
+            copy_rz(w, k).wait_recv()
             total += zrecv[w, k - 1].astype(f32)
         grad_ref[w] = -scale * total
 
     last = walkers - 1
+    for w in range(walkers):
+        offer(w)
     gather_z(0)
     if walkers > 1:
         gather_z(1)
     gather_y(0)
     gather_c(0)
-    for w in range(walkers):
+    for i in range(loads):
+        load(i).wait()
+
+    @pl.loop(0, walkers)
+    def _(w):
         make_tmat(w)
-        if w > 0:
+
+        @pl.when(w > 0)
+        def _():
             reduce_y(w - 1)
-        if w > 1:
+
+        @pl.when(w > 1)
+        def _():
             finish(w - 2)
-        if w + 2 < walkers:
+
+        @pl.when(w + 2 < walkers)
+        def _():
             gather_z(w + 2)
-        if w + 1 < walkers:
+
+        @pl.when(w + 1 < walkers)
+        def _():
             gather_y(w + 1)
+
         make_grad(w)
-        if w == last:
-            ec = send(eparts, erecv_c, ec_sem.at[0], ec_sem.at[1], over_c)
-        reduce_c(w)
-        if w > 0:
+        copy_rc(w).start()
+
+        @pl.when(w > 0)
+        def _():
             reduce_z(w - 1)
-        if w + 1 < walkers:
+
+        @pl.when(w + 1 < walkers)
+        def _():
             gather_c(w + 1)
+
+    ec = remote(eparts, erecv_c, ec_sem.at[0], ec_sem.at[1], over_c)
+    ec.start()
     ec.wait_recv()
     eyparts[...] = eparts[...] + erecv_c[...]
-    ey = send(eyparts, erecv_y, ey_sem.at[0], ey_sem.at[1], over_y)
+    ey = remote(eyparts, erecv_y, ey_sem.at[0], ey_sem.at[1], over_y)
+    ey.start()
     reduce_y(last)
     if last > 0:
         finish(last - 1)
     ey.wait_recv()
     ezparts[...] = eyparts[...] + erecv_y[...]
     ez = [
-        send(ezparts, erecv_z.at[k - 1], ez_send.at[k - 1], ez_recv.at[k - 1], over_z[k - 1])
+        remote(ezparts, erecv_z.at[k - 1], ez_send.at[k - 1], ez_recv.at[k - 1], over_z[k - 1])
         for k in range(1, planes)
     ]
+    for copy in ez:
+        copy.start()
     reduce_z(last)
     esum = ezparts[...]
     for k in range(1, planes):
         ez[k - 1].wait_recv()
         esum += erecv_z[k - 1]
-    energy_ref[...] = -0.5 * scale * esum
+    for w in range(walkers):
+        energy_ref[w] = -0.5 * scale * jnp.sum(esum[w])
     finish(last)
-    for copy in sent:
+    for copy in [ec, ey] + ez:
         copy.wait_send()
+
+    @pl.loop(0, walkers)
+    def _(w):
+        for k in range(1, planes):
+            copy_gz(w, k).wait_send()
+            copy_rz(w, k).wait_send()
+        for k in range(planes):
+            copy_gy(w, k).wait_send()
+        for k in range(COLUMNS):
+            copy_gc(w, k).wait_send()
+        copy_rc(w).wait_send()
+        copy_ry(w).wait_send()
 
 
 def per_device_kernel(green, chol_vecs, cotangent):
@@ -222,18 +256,18 @@
     dma = pltpu.SemaphoreType.DMA
     others = planes - 1
     estack = (walkers, 8, 128)
-    energy_parts, own_rows = pl.pallas_call(
+    energy, own_rows = pl.pallas_call(
         functools.partial(exchange_kernel, scale),
         out_shape=(
-            jax.ShapeDtypeStruct(estack, f32),
+            jax.ShapeDtypeStruct((walkers,), f32),
             jax.ShapeDtypeStruct((walkers,) + block, f32),
         ),
         in_specs=[
-            pl.BlockSpec(memory_space=pl.ANY),
-            pl.BlockSpec(memory_space=pl.ANY),
+            pl.BlockSpec(memory_space=pltpu.HBM),
+            pl.BlockSpec(memory_space=pltpu.HBM),
         ],
         out_specs=(
-            pl.BlockSpec(memory_space=pltpu.VMEM),
+            pl.BlockSpec(memory_space=pltpu.SMEM),
             pl.BlockSpec(memory_space=pltpu.VMEM),
         ),
         scratch_shapes=[
@@ -265,7 +299,7 @@
             dma((others,)), dma((others,)),
         ],
         compiler_params=pltpu.CompilerParams(
-            collective_id=0, has_side_effects=True, vmem_limit_bytes=60 * 1024 * 1024
+            collective_id=0, has_side_effects=True, vmem_limit_bytes=48 * 1024 * 1024
         ),
         cost_estimate=pl.CostEstimate(
             flops=4 * walkers * count * occupied * occupied * basis,
@@ -273,7 +307,6 @@
             transcendentals=0,
         ),
     )(green, chol_vecs)
-    energy = jnp.sum(energy_parts, axis=(1, 2))
     grad_green = cotangent[:, None, None] * own_rows
     return (energy, grad_green)
 

time: 60.6 us -> 59.7 us (0.985)
  other arithmetic: 3.08 us -> 0.79 us
  local copies, waits for them, and re-layouts: 0.01 us -> 1.41 us
    unnamed x2 -> x5, local copies, waits for them, and re-layouts: 0.01 us -> 1.41 us
    reduce_sum x1 -> x0, other arithmetic: 1.34 us -> none  [per_device_kernel(): energy = jnp.sum(energy_parts, axis=(1, 2))]
    mul x1, other arithmetic: 1.74 us -> 0.79 us  [per_device_kernel(): grad_green = cotangent[:, None, None] * own_rows]
where the time goes in v4:
time: 59.7 us; the launch traced here: 59.6 us
  Pallas kernels  56.7 us (95%)
  local copies, waits for them, and re-layouts  1.41 us (2%)
  other arithmetic  0.79 us (1%)
  between operations  0.66 us (1%)
    pallas_call x1, Pallas kernels, per_device_kernel(): pl.pallas_call(functools.partial(exchange_kernel, scale), out_shape=(jax....  56.7 us
    unnamed x5, local copies, waits for them, and re-layouts  1.41 us

profile of v4, /device:TPU:0, one launch (start us, length us, event | category | flops | bytes accessed | tf_op | source)
XLA Modules:
  0.0 59.6 jit_solution(2245588592434968125)
XLA Ops:
  0.6 0.0 copy-start
  0.6 0.9 %copy-done = bf16[4,16,1024]{2,1,0:T(8,128)(2,1)S(1)} copy-done((bf16[4,16,1024]{2,1,0:T(8,128)(2,1)S(1)}, bf16[4,16,1024]{2,1,0:T(8,128)(2,1)}, u32[]{:S(2)}) %copy-start) | copy-done | bytes 131096
  1.5 0.0 copy-start.1
  1.5 56.7 %shard_map.50 = (f32[4]{0:T(128)S(1)}, f32[4,16,1024]{2,1,0:T(8,128)S(1)}) custom-call(bf16[4,16,1024]{2,1,0:T(8,128)(2,1)S(1)} %copy-done, bf16[12,256,1024]{2,1,0:T(8,128)(2,1)} %chol_ref.1), custom_call_target="tpu_custom_call" | custom-call | flops 12884901888 | bytes 6291456 | tf_op jit(solution)/shard_map/pallas_call | solution.py:259
  58.3 0.0 copy-done.1
  58.3 0.8 %broadcast_multiply_fusion = f32[4,16,1024]{2,1,0:T(8,128)} fusion(f32[4,16,1024]{2,1,0:T(8,128)S(1)} %get-tuple-element.5, f32[4]{0:T(128)S(1)} %copy-done.1), kind=kLoop, calls=%fused_computation | loop fusion | flops 65536 | bytes 524304 | tf_op jit(solution)/shard_map/mul | solution.py:310
  59.1 0.5 copy.6
Async XLA Ops:
  0.6 0.9 %copy-start = (bf16[4,16,1024]{2,1,0:T(8,128)(2,1)S(1)}, bf16[4,16,1024]{2,1,0:T(8,128)(2,1)}, u32[]{:S(2)}) copy-start(bf16[4,16,1024]{2,1,0:T(8,128)(2,1)} %green_ref.1) | copy-start | bytes 393220
  1.5 56.8 %copy-start.1 = (f32[4]{0:T(128)S(1)}, f32[4]{0:T(128)}, u32[]{:S(2)}) copy-start(f32[4]{0:T(128)} %param.5) | copy-start | bytes 52

commit v5 on v4

--- a/solution.py
+++ b/solution.py
@@ -77,15 +77,15 @@
         column = full.at[w, :, y if k == 0 else 1 - y, c]
         return remote(column, column, gc_send.at[w, k], gc_recv.at[w, k], over_c)
 
-    def copy_rc(w):
-        return remote(partial.at[w, 1 - c], pair.at[w], rc_send.at[w], rc_recv.at[w], over_c)
-
-    def copy_ry(w):
-        return remote(ysend.at[w], yrecv.at[w], ry_send.at[w], ry_recv.at[w], over_y)
-
-    def copy_rz(w, k):
+    def copy_rc(u):
+        return remote(partial.at[u, 1 - c], pair.at[u], rc_send.at[u], rc_recv.at[u], over_c)
+
+    def copy_ry(u):
+        return remote(ysend.at[u], yrecv.at[u], ry_send.at[u], ry_recv.at[u], over_y)
+
+    def copy_rz(u, k):
         return remote(
-            zsend.at[w, plane[k]], zrecv.at[w, k - 1], rz_send.at[w, k - 1], rz_recv.at[w, k - 1], over_z[k - 1]
+            zsend.at[u, plane[k]], zrecv.at[u, k - 1], rz_send.at[u, k - 1], rz_recv.at[u, k - 1], over_z[k - 1]
         )
 
     def offer(w):
@@ -108,6 +108,41 @@
     def gather_c(w):
         for k in range(COLUMNS):
             copy_gc(w, k).wait_recv()
+
+    units, chunk = partial.shape[0], partial.shape[-1]
+    chunks = basis // chunk
+    period = loads + chunks
+
+    def reduce_y(u):
+        copy_rc(u).wait_recv()
+        ysend[u] = (partial[u, c, 1 - y] + pair[u, 1 - y]).astype(bf16)
+        copy_ry(u).start()
+        kept[u] = partial[u, c, y] + pair[u, y]
+
+    def reduce_z(u):
+        copy_ry(u).wait_recv()
+        zsend[u] = (kept[u] + yrecv[u].astype(f32)).astype(bf16)
+        for k in range(planes - 1, 0, -1):
+            copy_rz(u, k).start()
+        final[u] = kept[u, z] + yrecv[u, z].astype(f32)
+
+    def finish(u):
+        total = final[u]
+        for k in range(1, planes):
+            copy_rz(u, k).wait_recv()
+            total += zrecv[u, k - 1].astype(f32)
+        at = pl.multiple_of(lax.rem(u, chunks) * chunk, chunk)
+        grad_ref[u // chunks, :, pl.ds(at, chunk)] = -scale * total
+
+    def service(tick):
+        for lag, stage in ((2, reduce_y), (6, reduce_z), (10, finish)):
+            made = tick - lag
+            place = lax.rem(made + 2 * period, period) - loads
+            unit = (made + 2 * period) // period * chunks - 2 * chunks + place
+
+            @pl.when((place >= 0) & (unit >= 0) & (unit < units))
+            def _():
+                stage(unit)
 
     def make_tmat(w):
         @pl.loop(0, loads)
@@ -119,13 +154,12 @@
             for j in range(per):
                 at = pl.multiple_of((first + j) * occupied, occupied)
                 half[:, pl.ds(at, occupied)] = tmat[j * occupied:(j + 1) * occupied].astype(bf16)
-
-    chunk = 256 if basis % 256 == 0 else 128
+            service(w * period + i)
 
     def make_grad(w):
         eparts[w] = jnp.zeros(eparts.shape[1:], f32)
 
-        @pl.loop(0, basis // chunk)
+        @pl.loop(0, chunks)
         def _(i):
             at = pl.multiple_of(i * chunk, chunk)
             right = vecs[:, :, pl.ds(at, chunk)].reshape(count * occupied, chunk)
@@ -138,35 +172,16 @@
                 for yy in range(COLUMNS):
                     for cc in range(CORES):
                         row = ((zz * COLUMNS + yy) * CORES + cc) * rows
-                        partial[w, cc, yy, zz, :, pl.ds(at, chunk)] = part[row:row + rows]
-
-    def reduce_y(w):
-        copy_rc(w).wait_recv()
-        ysend[w] = (partial[w, c, 1 - y] + pair[w, 1 - y]).astype(bf16)
-        copy_ry(w).start()
-        kept[w] = partial[w, c, y] + pair[w, y]
-
-    def reduce_z(w):
-        copy_ry(w).wait_recv()
-        zsend[w] = (kept[w] + yrecv[w].astype(f32)).astype(bf16)
-        for k in range(planes - 1, 0, -1):
-            copy_rz(w, k).start()
-        final[w] = kept[w, z] + yrecv[w, z].astype(f32)
-
-    def finish(w):
-        total = final[w]
-        for k in range(1, planes):
-            copy_rz(w, k).wait_recv()
-            total += zrecv[w, k - 1].astype(f32)
-        grad_ref[w] = -scale * total
-
-    last = walkers - 1
+                        partial[w * chunks + i, cc, yy, zz] = part[row:row + rows]
+            copy_rc(w * chunks + i).start()
+            service(w * period + loads + i)
+
     for w in range(walkers):
         offer(w)
     gather_z(0)
+    gather_y(0)
     if walkers > 1:
         gather_z(1)
-    gather_y(0)
     gather_c(0)
     for i in range(loads):
         load(i).wait()
@@ -175,14 +190,6 @@
     def _(w):
         make_tmat(w)
 
-        @pl.when(w > 0)
-        def _():
-            reduce_y(w - 1)
-
-        @pl.when(w > 1)
-        def _():
-            finish(w - 2)
-
         @pl.when(w + 2 < walkers)
         def _():
             gather_z(w + 2)
@@ -192,25 +199,28 @@
             gather_y(w + 1)
 
         make_grad(w)
-        copy_rc(w).start()
-
-        @pl.when(w > 0)
-        def _():
-            reduce_z(w - 1)
 
         @pl.when(w + 1 < walkers)
         def _():
             gather_c(w + 1)
 
+    end = walkers * period
     ec = remote(eparts, erecv_c, ec_sem.at[0], ec_sem.at[1], over_c)
     ec.start()
+
+    @pl.loop(end, end + 2)
+    def _(tick):
+        service(tick)
+
     ec.wait_recv()
     eyparts[...] = eparts[...] + erecv_c[...]
     ey = remote(eyparts, erecv_y, ey_sem.at[0], ey_sem.at[1], over_y)
     ey.start()
-    reduce_y(last)
-    if last > 0:
-        finish(last - 1)
+
+    @pl.loop(end + 2, end + 6)
+    def _(tick):
+        service(tick)
+
     ey.wait_recv()
     ezparts[...] = eyparts[...] + erecv_y[...]
     ez = [
@@ -219,14 +229,17 @@
     ]
     for copy in ez:
         copy.start()
-    reduce_z(last)
+
+    @pl.loop(end + 6, end + 10)
+    def _(tick):
+        service(tick)
+
     esum = ezparts[...]
     for k in range(1, planes):
         ez[k - 1].wait_recv()
         esum += erecv_z[k - 1]
     for w in range(walkers):
         energy_ref[w] = -0.5 * scale * jnp.sum(esum[w])
-    finish(last)
     for copy in [ec, ey] + ez:
         copy.wait_send()
 
@@ -234,13 +247,17 @@
     def _(w):
         for k in range(1, planes):
             copy_gz(w, k).wait_send()
-            copy_rz(w, k).wait_send()
         for k in range(planes):
             copy_gy(w, k).wait_send()
         for k in range(COLUMNS):
             copy_gc(w, k).wait_send()
-        copy_rc(w).wait_send()
-        copy_ry(w).wait_send()
+
+    @pl.loop(0, units)
+    def _(u):
+        copy_rc(u).wait_send()
+        copy_ry(u).wait_send()
+        for k in range(1, planes):
+            copy_rz(u, k).wait_send()
 
 
 def per_device_kernel(green, chol_vecs, cotangent):
@@ -253,6 +270,9 @@
     loads = count // per
     bf16, f32 = jnp.bfloat16, jnp.float32
     block = (rows, basis)
+    chunk = 256 if basis % 256 == 0 else 128
+    units = walkers * (basis // chunk)
+    piece = (rows, chunk)
     dma = pltpu.SemaphoreType.DMA
     others = planes - 1
     estack = (walkers, 8, 128)
@@ -274,14 +294,14 @@
             pltpu.VMEM((count, occupied, basis), bf16),
             pltpu.VMEM((walkers, planes, COLUMNS, CORES) + block, bf16),
             pltpu.VMEM((occupied, count * occupied), bf16),
-            pltpu.VMEM((walkers, CORES, COLUMNS, planes) + block, f32),
-            pltpu.VMEM((walkers, COLUMNS, planes) + block, f32),
-            pltpu.VMEM((walkers, planes) + block, bf16),
-            pltpu.VMEM((walkers, planes) + block, bf16),
-            pltpu.VMEM((walkers, planes) + block, f32),
-            pltpu.VMEM((walkers, planes) + block, bf16),
-            pltpu.VMEM((walkers, others) + block, bf16),
-            pltpu.VMEM((walkers,) + block, f32),
+            pltpu.VMEM((units, CORES, COLUMNS, planes) + piece, f32),
+            pltpu.VMEM((units, COLUMNS, planes) + piece, f32),
+            pltpu.VMEM((units, planes) + piece, bf16),
+            pltpu.VMEM((units, planes) + piece, bf16),
+            pltpu.VMEM((units, planes) + piece, f32),
+            pltpu.VMEM((units, planes) + piece, bf16),
+            pltpu.VMEM((units, others) + piece, bf16),
+            pltpu.VMEM((units,) + piece, f32),
             pltpu.VMEM(estack, f32),
             pltpu.VMEM(estack, f32),
             pltpu.VMEM(estack, f32),
@@ -292,9 +312,9 @@
             dma((walkers, others)), dma((walkers, others)),
             dma((walkers, planes)), dma((walkers, planes)),
             dma((walkers, COLUMNS)), dma((walkers, COLUMNS)),
-            dma((walkers,)), dma((walkers,)),
-            dma((walkers,)), dma((walkers,)),
-            dma((walkers, others)), dma((walkers, others)),
+            dma((units,)), dma((units,)),
+            dma((units,)), dma((units,)),
+            dma((units, others)), dma((units, others)),
             dma((2,)), dma((2,)),
             dma((others,)), dma((others,)),
         ],

time: 59.7 us -> 56.3 us (0.943)
  Pallas kernels: 56.7 us -> 53.3 us
    pallas_call x1, Pallas kernels: 56.7 us -> 53.3 us  [per_device_kernel(): pl.pallas_call(functools.partial(exchange_kernel, scale), out_shape=(jax....]
where the time goes in v5:
time: 56.3 us; the launch traced here: 56.2 us
  Pallas kernels  53.3 us (95%)
  local copies, waits for them, and re-layouts  1.41 us (3%)
  other arithmetic  0.79 us (1%)
  between operations  0.66 us (1%)
    pallas_call x1, Pallas kernels, per_device_kernel(): pl.pallas_call(functools.partial(exchange_kernel, scale), out_shape=(jax....  53.3 us
    unnamed x5, local copies, waits for them, and re-layouts  1.41 us

profile of v5, /device:TPU:0, one launch (start us, length us, event | category | flops | bytes accessed | tf_op | source)
XLA Modules:
  0.0 56.2 jit_solution(8871062318161955865)
XLA Ops:
  0.6 0.0 copy-start
  0.6 0.9 %copy-done = bf16[4,16,1024]{2,1,0:T(8,128)(2,1)S(1)} copy-done((bf16[4,16,1024]{2,1,0:T(8,128)(2,1)S(1)}, bf16[4,16,1024]{2,1,0:T(8,128)(2,1)}, u32[]{:S(2)}) %copy-start) | copy-done | bytes 131096
  1.5 0.0 copy-start.1
  1.5 53.3 %shard_map.50 = (f32[4]{0:T(128)S(1)}, f32[4,16,1024]{2,1,0:T(8,128)S(1)}) custom-call(bf16[4,16,1024]{2,1,0:T(8,128)(2,1)S(1)} %copy-done, bf16[12,256,1024]{2,1,0:T(8,128)(2,1)} %chol_ref.1), custom_call_target="tpu_custom_call" | custom-call | flops 12884901888 | bytes 6291456 | tf_op jit(solution)/shard_map/pallas_call | solution.py:279
  54.8 0.0 copy-done.1
  54.9 0.8 %broadcast_multiply_fusion = f32[4,16,1024]{2,1,0:T(8,128)} fusion(f32[4,16,1024]{2,1,0:T(8,128)S(1)} %get-tuple-element.5, f32[4]{0:T(128)S(1)} %copy-done.1), kind=kLoop, calls=%fused_computation | loop fusion | flops 65536 | bytes 524304 | tf_op jit(solution)/shard_map/mul | solution.py:330
  55.6 0.5 copy.6
Async XLA Ops:
  0.6 0.9 %copy-start = (bf16[4,16,1024]{2,1,0:T(8,128)(2,1)S(1)}, bf16[4,16,1024]{2,1,0:T(8,128)(2,1)}, u32[]{:S(2)}) copy-start(bf16[4,16,1024]{2,1,0:T(8,128)(2,1)} %green_ref.1) | copy-start | bytes 393220
  1.5 53.3 %copy-start.1 = (f32[4]{0:T(128)S(1)}, f32[4]{0:T(128)}, u32[]{:S(2)}) copy-start(f32[4]{0:T(128)} %param.5) | copy-start | bytes 52

commit v6 on v5

--- a/solution.py
+++ b/solution.py
@@ -109,9 +109,13 @@
         for k in range(COLUMNS):
             copy_gc(w, k).wait_recv()
 
+    wide = half.shape[0]
     units, chunk = partial.shape[0], partial.shape[-1]
     chunks = basis // chunk
-    period = loads + chunks
+    split = 2 if chunks % 2 == 0 else 1
+    steps = wide * chunks // split
+    period = loads + steps
+    lags = (1, 3, 5)
 
     def reduce_y(u):
         copy_rc(u).wait_recv()
@@ -135,80 +139,90 @@
         grad_ref[u // chunks, :, pl.ds(at, chunk)] = -scale * total
 
     def service(tick):
-        for lag, stage in ((2, reduce_y), (6, reduce_z), (10, finish)):
-            made = tick - lag
-            place = lax.rem(made + 2 * period, period) - loads
-            unit = (made + 2 * period) // period * chunks - 2 * chunks + place
-
-            @pl.when((place >= 0) & (unit >= 0) & (unit < units))
+        for lag, stage in zip(lags, (reduce_y, reduce_z, finish)):
+            made = tick - lag + 2 * period
+            place = lax.rem(made, period) - loads
+            step = (made // period - 2) * steps + place
+
+            @pl.when((place >= 0) & (step >= 0) & (step < units // split))
             def _():
-                stage(unit)
-
-    def make_tmat(w):
+                for j in range(split):
+                    stage(step * split + j)
+
+    def make_tmat(group):
         @pl.loop(0, loads)
         def _(i):
             first = i * per
             left = vecs[pl.ds(first, per)].reshape(per * occupied, basis)
-            right = full[w].reshape(occupied, basis)
+            right = full[pl.ds(group * wide, wide)].reshape(wide * occupied, basis)
             tmat = lax.dot_general(left, right, (((1,), (1,)), ((), ())), preferred_element_type=f32)
             for j in range(per):
                 at = pl.multiple_of((first + j) * occupied, occupied)
-                half[:, pl.ds(at, occupied)] = tmat[j * occupied:(j + 1) * occupied].astype(bf16)
-            service(w * period + i)
-
-    def make_grad(w):
-        eparts[w] = jnp.zeros(eparts.shape[1:], f32)
-
-        @pl.loop(0, chunks)
+                for v in range(wide):
+                    one = tmat[j * occupied:(j + 1) * occupied, v * occupied:(v + 1) * occupied]
+                    half[v, :, pl.ds(at, occupied)] = one.astype(bf16)
+            service(group * period + i)
+
+    def make_grad(group):
+        for v in range(wide):
+            eparts[group * wide + v] = jnp.zeros(eparts.shape[1:], f32)
+
+        @pl.loop(0, steps)
         def _(i):
-            at = pl.multiple_of(i * chunk, chunk)
-            right = vecs[:, :, pl.ds(at, chunk)].reshape(count * occupied, chunk)
-            part = jnp.dot(half[...], right, preferred_element_type=f32)
-            green = full[w, :, :, :, :, pl.ds(at, chunk)].reshape(occupied, chunk)
-            folded = (part * green.astype(f32)).reshape(occupied // 8, 8, chunk).sum(axis=0)
-            for lane in range(0, chunk, 128):
-                eparts[w] += folded[:, lane:lane + 128]
-            for zz in range(planes):
-                for yy in range(COLUMNS):
-                    for cc in range(CORES):
-                        row = ((zz * COLUMNS + yy) * CORES + cc) * rows
-                        partial[w * chunks + i, cc, yy, zz] = part[row:row + rows]
-            copy_rc(w * chunks + i).start()
-            service(w * period + loads + i)
+            v = i * split // chunks
+            w = group * wide + v
+            size = split * chunk
+            at = pl.multiple_of(lax.rem(i * split, chunks) * chunk, size)
+            right = vecs[:, :, pl.ds(at, size)].reshape(count * occupied, size)
+            part = jnp.dot(half[v], right, preferred_element_type=f32)
+            green = full[w, :, :, :, :, pl.ds(at, size)].reshape(occupied, size)
+            folded = (part * green.astype(f32)).reshape(occupied // 8, 8, size).sum(axis=0)
+            eparts[w] += sum(folded[:, lane:lane + 128] for lane in range(0, size, 128))
+            step = group * steps + i
+            for j in range(split):
+                for zz in range(planes):
+                    for yy in range(COLUMNS):
+                        for cc in range(CORES):
+                            row = ((zz * COLUMNS + yy) * CORES + cc) * rows
+                            partial[step * split + j, cc, yy, zz] = part[row:row + rows, j * chunk:(j + 1) * chunk]
+                copy_rc(step * split + j).start()
+            service(group * period + loads + i)
 
     for w in range(walkers):
         offer(w)
-    gather_z(0)
-    gather_y(0)
-    if walkers > 1:
-        gather_z(1)
-    gather_c(0)
+    for w in range(wide):
+        gather_z(w)
+    for w in range(wide):
+        gather_y(w)
+    for w in range(wide):
+        gather_c(w)
     for i in range(loads):
         load(i).wait()
-
-    @pl.loop(0, walkers)
-    def _(w):
-        make_tmat(w)
-
-        @pl.when(w + 2 < walkers)
+    groups = walkers // wide
+
+    @pl.loop(0, groups)
+    def _(group):
+        make_tmat(group)
+
+        @pl.when(group + 1 < groups)
         def _():
-            gather_z(w + 2)
-
-        @pl.when(w + 1 < walkers)
+            for v in range(wide):
+                gather_z((group + 1) * wide + v)
+            for v in range(wide):
+                gather_y((group + 1) * wide + v)
+
+        make_grad(group)
+
+        @pl.when(group + 1 < groups)
         def _():
-            gather_y(w + 1)
-
-        make_grad(w)
-
-        @pl.when(w + 1 < walkers)
-        def _():
-            gather_c(w + 1)
-
-    end = walkers * period
+            for v in range(wide):
+                gather_c((group + 1) * wide + v)
+
+    end = groups * period
     ec = remote(eparts, erecv_c, ec_sem.at[0], ec_sem.at[1], over_c)
     ec.start()
 
-    @pl.loop(end, end + 2)
+    @pl.loop(end, end + lags[0])
     def _(tick):
         service(tick)
 
@@ -217,7 +231,7 @@
     ey = remote(eyparts, erecv_y, ey_sem.at[0], ey_sem.at[1], over_y)
     ey.start()
 
-    @pl.loop(end + 2, end + 6)
+    @pl.loop(end + lags[0], end + lags[1])
     def _(tick):
         service(tick)
 
@@ -230,7 +244,7 @@
     for copy in ez:
         copy.start()
 
-    @pl.loop(end + 6, end + 10)
+    @pl.loop(end + lags[1], end + lags[2])
     def _(tick):
         service(tick)
 
@@ -272,6 +286,7 @@
     block = (rows, basis)
     chunk = 256 if basis % 256 == 0 else 128
     units = walkers * (basis // chunk)
+    wide = 2 if walkers % 2 == 0 else 1
     piece = (rows, chunk)
     dma = pltpu.SemaphoreType.DMA
     others = planes - 1
@@ -293,7 +308,7 @@
         scratch_shapes=[
             pltpu.VMEM((count, occupied, basis), bf16),
             pltpu.VMEM((walkers, planes, COLUMNS, CORES) + block, bf16),
-            pltpu.VMEM((occupied, count * occupied), bf16),
+            pltpu.VMEM((wide, occupied, count * occupied), bf16),
             pltpu.VMEM((units, CORES, COLUMNS, planes) + piece, f32),
             pltpu.VMEM((units, COLUMNS, planes) + piece, f32),
             pltpu.VMEM((units, planes) + piece, bf16),

time: 56.3 us -> 63.5 us (1.13)
  Pallas kernels: 53.3 us -> 60.5 us
    pallas_call x1, Pallas kernels: 53.3 us -> 60.5 us  [per_device_kernel(): pl.pallas_call(functools.partial(exchange_kernel, scale), out_shape=(jax....]
where the time goes in v6:
time: 63.5 us; the launch traced here: 63.4 us
  Pallas kernels  60.5 us (95%)
  local copies, waits for them, and re-layouts  1.41 us (2%)
  other arithmetic  0.79 us (1%)
  between operations  0.66 us (1%)
    pallas_call x1, Pallas kernels, per_device_kernel(): pl.pallas_call(functools.partial(exchange_kernel, scale), out_shape=(jax....  60.5 us
    unnamed x5, local copies, waits for them, and re-layouts  1.41 us

profile of v6, /device:TPU:0, one launch (start us, length us, event | category | flops | bytes accessed | tf_op | source)
XLA Modules:
  0.0 63.4 jit_solution(8028640892412998195)
XLA Ops:
  0.6 0.0 copy-start
  0.6 0.9 %copy-done = bf16[4,16,1024]{2,1,0:T(8,128)(2,1)S(1)} copy-done((bf16[4,16,1024]{2,1,0:T(8,128)(2,1)S(1)}, bf16[4,16,1024]{2,1,0:T(8,128)(2,1)}, u32[]{:S(2)}) %copy-start) | copy-done | bytes 131096
  1.5 0.0 copy-start.1
  1.5 60.5 %shard_map.50 = (f32[4]{0:T(128)S(1)}, f32[4,16,1024]{2,1,0:T(8,128)S(1)}) custom-call(bf16[4,16,1024]{2,1,0:T(8,128)(2,1)S(1)} %copy-done, bf16[12,256,1024]{2,1,0:T(8,128)(2,1)} %chol_ref.1), custom_call_target="tpu_custom_call" | custom-call | flops 12884901888 | bytes 6291456 | tf_op jit(solution)/shard_map/pallas_call | solution.py:294
  62.1 0.0 copy-done.1
  62.1 0.8 %broadcast_multiply_fusion = f32[4,16,1024]{2,1,0:T(8,128)} fusion(f32[4,16,1024]{2,1,0:T(8,128)S(1)} %get-tuple-element.5, f32[4]{0:T(128)S(1)} %copy-done.1), kind=kLoop, calls=%fused_computation | loop fusion | flops 65536 | bytes 524304 | tf_op jit(solution)/shard_map/mul | solution.py:345
  62.9 0.5 copy.6
Async XLA Ops:
  0.6 0.9 %copy-start = (bf16[4,16,1024]{2,1,0:T(8,128)(2,1)S(1)}, bf16[4,16,1024]{2,1,0:T(8,128)(2,1)}, u32[]{:S(2)}) copy-start(bf16[4,16,1024]{2,1,0:T(8,128)(2,1)} %green_ref.1) | copy-start | bytes 393220
  1.5 60.5 %copy-start.1 = (f32[4]{0:T(128)S(1)}, f32[4]{0:T(128)}, u32[]{:S(2)}) copy-start(f32[4]{0:T(128)} %param.5) | copy-start | bytes 52

commit v7 on v5

--- a/solution.py
+++ b/solution.py
@@ -15,7 +15,7 @@
     scale,
     green_ref, chol_ref,
     energy_ref, grad_ref,
-    vecs, full, half, partial, pair, ysend, yrecv, kept, zsend, zrecv, final,
+    vecs, full, turned, half, partial, pair, ysend, yrecv, kept, zsend, zrecv, final,
     eparts, eyparts, ezparts, erecv_c, erecv_y, erecv_z,
     load_sem, own_sem, gz_send, gz_recv, gy_send, gy_recv, gc_send, gc_recv,
     rc_send, rc_recv, ry_send, ry_recv, rz_send, rz_recv,
@@ -145,12 +145,13 @@
                 stage(unit)
 
     def make_tmat(w):
+        turned[...] = full[w].reshape(occupied, basis).T
+
         @pl.loop(0, loads)
         def _(i):
             first = i * per
             left = vecs[pl.ds(first, per)].reshape(per * occupied, basis)
-            right = full[w].reshape(occupied, basis)
-            tmat = lax.dot_general(left, right, (((1,), (1,)), ((), ())), preferred_element_type=f32)
+            tmat = jnp.dot(left, turned[...], preferred_element_type=f32)
             for j in range(per):
                 at = pl.multiple_of((first + j) * occupied, occupied)
                 half[:, pl.ds(at, occupied)] = tmat[j * occupied:(j + 1) * occupied].astype(bf16)
@@ -293,6 +294,7 @@
         scratch_shapes=[
             pltpu.VMEM((count, occupied, basis), bf16),
             pltpu.VMEM((walkers, planes, COLUMNS, CORES) + block, bf16),
+            pltpu.VMEM((basis, occupied), bf16),
             pltpu.VMEM((occupied, count * occupied), bf16),
             pltpu.VMEM((units, CORES, COLUMNS, planes) + piece, f32),
             pltpu.VMEM((units, COLUMNS, planes) + piece, f32),

time: 56.3 us -> 56.6 us (level)
  no operation moved by 1% of the time
where the time goes in v7:
time: 56.6 us; the launch traced here: 56.4 us
  Pallas kernels  53.5 us (95%)
  local copies, waits for them, and re-layouts  1.41 us (2%)
  other arithmetic  0.79 us (1%)
  between operations  0.66 us (1%)
    pallas_call x1, Pallas kernels, per_device_kernel(): pl.pallas_call(functools.partial(exchange_kernel, scale), out_shape=(jax....  53.5 us
    unnamed x5, local copies, waits for them, and re-layouts  1.41 us

profile of v7, /device:TPU:0, one launch (start us, length us, event | category | flops | bytes accessed | tf_op | source)
XLA Modules:
  0.0 56.4 jit_solution(4463388782433268771)
XLA Ops:
  0.6 0.0 copy-start
  0.6 0.9 %copy-done = bf16[4,16,1024]{2,1,0:T(8,128)(2,1)S(1)} copy-done((bf16[4,16,1024]{2,1,0:T(8,128)(2,1)S(1)}, bf16[4,16,1024]{2,1,0:T(8,128)(2,1)}, u32[]{:S(2)}) %copy-start) | copy-done | bytes 131096
  1.5 0.0 copy-start.1
  1.5 53.5 %shard_map.50 = (f32[4]{0:T(128)S(1)}, f32[4,16,1024]{2,1,0:T(8,128)S(1)}) custom-call(bf16[4,16,1024]{2,1,0:T(8,128)(2,1)S(1)} %copy-done, bf16[12,256,1024]{2,1,0:T(8,128)(2,1)} %chol_ref.1), custom_call_target="tpu_custom_call" | custom-call | flops 12884901888 | bytes 6291456 | tf_op jit(solution)/shard_map/pallas_call | solution.py:280
  55.1 0.0 copy-done.1
  55.1 0.8 %broadcast_multiply_fusion = f32[4,16,1024]{2,1,0:T(8,128)} fusion(f32[4,16,1024]{2,1,0:T(8,128)S(1)} %get-tuple-element.5, f32[4]{0:T(128)S(1)} %copy-done.1), kind=kLoop, calls=%fused_computation | loop fusion | flops 65536 | bytes 524304 | tf_op jit(solution)/shard_map/mul | solution.py:332
  55.9 0.5 copy.6
Async XLA Ops:
  0.6 0.9 %copy-start = (bf16[4,16,1024]{2,1,0:T(8,128)(2,1)S(1)}, bf16[4,16,1024]{2,1,0:T(8,128)(2,1)}, u32[]{:S(2)}) copy-start(bf16[4,16,1024]{2,1,0:T(8,128)(2,1)} %green_ref.1) | copy-start | bytes 393220
  1.5 53.6 %copy-start.1 = (f32[4]{0:T(128)S(1)}, f32[4]{0:T(128)}, u32[]{:S(2)}) copy-start(f32[4]{0:T(128)} %param.5) | copy-start | bytes 52

commit v8 on v5

--- a/solution.py
+++ b/solution.py
@@ -15,7 +15,7 @@
     scale,
     green_ref, chol_ref,
     energy_ref, grad_ref,
-    vecs, full, half, partial, pair, ysend, yrecv, kept, zsend, zrecv, final,
+    vecs, full, half, partial, csend, pair, ysend, yrecv, kept, zsend, zrecv, final,
     eparts, eyparts, ezparts, erecv_c, erecv_y, erecv_z,
     load_sem, own_sem, gz_send, gz_recv, gy_send, gy_recv, gc_send, gc_recv,
     rc_send, rc_recv, ry_send, ry_recv, rz_send, rz_recv,
@@ -78,7 +78,7 @@
         return remote(column, column, gc_send.at[w, k], gc_recv.at[w, k], over_c)
 
     def copy_rc(u):
-        return remote(partial.at[u, 1 - c], pair.at[u], rc_send.at[u], rc_recv.at[u], over_c)
+        return remote(csend.at[u, 1 - c], pair.at[u], rc_send.at[u], rc_recv.at[u], over_c)
 
     def copy_ry(u):
         return remote(ysend.at[u], yrecv.at[u], ry_send.at[u], ry_recv.at[u], over_y)
@@ -115,9 +115,9 @@
 
     def reduce_y(u):
         copy_rc(u).wait_recv()
-        ysend[u] = (partial[u, c, 1 - y] + pair[u, 1 - y]).astype(bf16)
+        ysend[u] = (partial[u, c, 1 - y] + pair[u, 1 - y].astype(f32)).astype(bf16)
         copy_ry(u).start()
-        kept[u] = partial[u, c, y] + pair[u, y]
+        kept[u] = partial[u, c, y] + pair[u, y].astype(f32)
 
     def reduce_z(u):
         copy_ry(u).wait_recv()
@@ -173,6 +173,7 @@
                     for cc in range(CORES):
                         row = ((zz * COLUMNS + yy) * CORES + cc) * rows
                         partial[w * chunks + i, cc, yy, zz] = part[row:row + rows]
+                        csend[w * chunks + i, cc, yy, zz] = part[row:row + rows].astype(bf16)
             copy_rc(w * chunks + i).start()
             service(w * period + loads + i)
 
@@ -295,7 +296,8 @@
             pltpu.VMEM((walkers, planes, COLUMNS, CORES) + block, bf16),
             pltpu.VMEM((occupied, count * occupied), bf16),
             pltpu.VMEM((units, CORES, COLUMNS, planes) + piece, f32),
-            pltpu.VMEM((units, COLUMNS, planes) + piece, f32),
+            pltpu.VMEM((units, CORES, COLUMNS, planes) + piece, bf16),
+            pltpu.VMEM((units, COLUMNS, planes) + piece, bf16),
             pltpu.VMEM((units, planes) + piece, bf16),
             pltpu.VMEM((units, planes) + piece, bf16),
             pltpu.VMEM((units, planes) + piece, f32),

time: 56.3 us -> 56.2 us (level)
  no operation moved by 1% of the time
where the time goes in v8:
time: 56.2 us; the launch traced here: 56 us
  Pallas kernels  53.2 us (95%)
  local copies, waits for them, and re-layouts  1.41 us (3%)
  other arithmetic  0.79 us (1%)
  between operations  0.66 us (1%)
    pallas_call x1, Pallas kernels, per_device_kernel(): pl.pallas_call(functools.partial(exchange_kernel, scale), out_shape=(jax....  53.2 us
    unnamed x5, local copies, waits for them, and re-layouts  1.41 us

profile of v8, /device:TPU:0, one launch (start us, length us, event | category | flops | bytes accessed | tf_op | source)
XLA Modules:
  0.0 56.0 jit_solution(6812217493969305736)
XLA Ops:
  0.6 0.0 copy-start
  0.6 0.9 %copy-done = bf16[4,16,1024]{2,1,0:T(8,128)(2,1)S(1)} copy-done((bf16[4,16,1024]{2,1,0:T(8,128)(2,1)S(1)}, bf16[4,16,1024]{2,1,0:T(8,128)(2,1)}, u32[]{:S(2)}) %copy-start) | copy-done | bytes 131096
  1.5 0.0 copy-start.1
  1.5 53.2 %shard_map.50 = (f32[4]{0:T(128)S(1)}, f32[4,16,1024]{2,1,0:T(8,128)S(1)}) custom-call(bf16[4,16,1024]{2,1,0:T(8,128)(2,1)S(1)} %copy-done, bf16[12,256,1024]{2,1,0:T(8,128)(2,1)} %chol_ref.1), custom_call_target="tpu_custom_call" | custom-call | flops 12884901888 | bytes 6291456 | tf_op jit(solution)/shard_map/pallas_call | solution.py:280
  54.7 0.0 copy-done.1
  54.7 0.8 %broadcast_multiply_fusion = f32[4,16,1024]{2,1,0:T(8,128)} fusion(f32[4,16,1024]{2,1,0:T(8,128)S(1)} %get-tuple-element.5, f32[4]{0:T(128)S(1)} %copy-done.1), kind=kLoop, calls=%fused_computation | loop fusion | flops 65536 | bytes 524304 | tf_op jit(solution)/shard_map/mul | solution.py:332
  55.5 0.5 copy.6
Async XLA Ops:
  0.6 0.9 %copy-start = (bf16[4,16,1024]{2,1,0:T(8,128)(2,1)S(1)}, bf16[4,16,1024]{2,1,0:T(8,128)(2,1)}, u32[]{:S(2)}) copy-start(bf16[4,16,1024]{2,1,0:T(8,128)(2,1)} %green_ref.1) | copy-start | bytes 393220
  1.5 53.2 %copy-start.1 = (f32[4]{0:T(128)S(1)}, f32[4]{0:T(128)}, u32[]{:S(2)}) copy-start(f32[4]{0:T(128)} %param.5) | copy-start | bytes 52

commit v9 on v5

--- a/solution.py
+++ b/solution.py
@@ -17,7 +17,7 @@
     energy_ref, grad_ref,
     vecs, full, half, partial, pair, ysend, yrecv, kept, zsend, zrecv, final,
     eparts, eyparts, ezparts, erecv_c, erecv_y, erecv_z,
-    load_sem, own_sem, gz_send, gz_recv, gy_send, gy_recv, gc_send, gc_recv,
+    load_sem, own_sem, gu_send, gu_recv, gd_send, gd_recv, gy_send, gy_recv, gc_send, gc_recv,
     rc_send, rc_recv, ry_send, ry_recv, rz_send, rz_recv,
     ec_sem, ey_sem, ez_send, ez_recv,
 ):
@@ -35,7 +35,6 @@
         return {"chol": (zz * COLUMNS + yy) * CORES + cc}
 
     plane = [lax.rem(z + k, planes) for k in range(planes)]
-    source = [lax.rem(z - k + planes, planes) for k in range(planes)]
     over_z = [device(plane[k], y, c) for k in range(1, planes)]
     over_y = device(z, 1 - y, c)
     over_c = device(z, y, 1 - c)
@@ -65,13 +64,20 @@
             device_id=peer, device_id_type=pl.DeviceIdType.MESH,
         )
 
-    def copy_gz(w, k):
-        block = full.at[w, z, y, c]
-        return remote(block, block, gz_send.at[w, k - 1], gz_recv.at[w, k - 1], over_z[k - 1])
-
-    def copy_gy(w, k):
-        block = full.at[w, source[k], y, c]
-        return remote(block, block, gy_send.at[w, k], gy_recv.at[w, k], over_y)
+    above = device(jnp.minimum(z + 1, planes - 1), y, c)
+    below = device(jnp.maximum(z - 1, 0), y, c)
+
+    def copy_up(w, h, s):
+        block = full.at[w, s, y, c]
+        return remote(block, block, gu_send.at[w, h - 1], gu_recv.at[w, h - 1], above)
+
+    def copy_down(w, h, s):
+        block = full.at[w, s, y, c]
+        return remote(block, block, gd_send.at[w, h - 1], gd_recv.at[w, h - 1], below)
+
+    def copy_gy(w, s):
+        block = full.at[w, s, y, c]
+        return remote(block, block, gy_send.at[w, s], gy_recv.at[w, s], over_y)
 
     def copy_gc(w, k):
         column = full.at[w, :, y if k == 0 else 1 - y, c]
@@ -90,14 +96,40 @@
 
     def offer(w):
         pltpu.make_async_copy(green_ref.at[w], full.at[w, z, y, c], own_sem.at[w]).wait()
-        for k in range(planes - 1, 0, -1):
-            copy_gz(w, k).start()
-        copy_gy(w, 0).start()
-
-    def gather_z(w):
-        for k in range(1, planes):
-            copy_gz(w, k).wait_recv()
-            copy_gy(w, k).start()
+        @pl.when(z + 1 < planes)
+        def _():
+            copy_up(w, 1, z).start()
+
+        @pl.when(z > 0)
+        def _():
+            copy_down(w, 1, z).start()
+
+        copy_gy(w, z).start()
+
+    def gather_hop(w, h):
+        @pl.when(z - h >= 0)
+        def _():
+            copy_up(w, h, z - h).wait_recv()
+
+            @pl.when(z + 1 < planes)
+            def _():
+                copy_up(w, h + 1, z - h).start()
+
+            copy_gy(w, z - h).start()
+
+        @pl.when(z + h < planes)
+        def _():
+            copy_down(w, h, z + h).wait_recv()
+
+            @pl.when(z > 0)
+            def _():
+                copy_down(w, h + 1, z + h).start()
+
+            copy_gy(w, z + h).start()
+
+    def gather_z(w, first=1):
+        for h in range(first, planes):
+            gather_hop(w, h)
         copy_gc(w, 0).start()
 
     def gather_y(w):
@@ -155,6 +187,11 @@
                 at = pl.multiple_of((first + j) * occupied, occupied)
                 half[:, pl.ds(at, occupied)] = tmat[j * occupied:(j + 1) * occupied].astype(bf16)
             service(w * period + i)
+
+            @pl.when((w + 2 < walkers) & (i + 1 < planes))
+            def _():
+                gather_hop(w + 2, i + 1)
+
 
     def make_grad(w):
         eparts[w] = jnp.zeros(eparts.shape[1:], f32)
@@ -192,7 +229,7 @@
 
         @pl.when(w + 2 < walkers)
         def _():
-            gather_z(w + 2)
+            gather_z(w + 2, loads + 1)
 
         @pl.when(w + 1 < walkers)
         def _():
@@ -245,8 +282,15 @@
 
     @pl.loop(0, walkers)
     def _(w):
-        for k in range(1, planes):
-            copy_gz(w, k).wait_send()
+        for h in range(1, planes):
+            @pl.when((z - (h - 1) >= 0) & (z + 1 < planes))
+            def _():
+                copy_up(w, h, z - (h - 1)).wait_send()
+
+            @pl.when((z + (h - 1) < planes) & (z > 0))
+            def _():
+                copy_down(w, h, z + (h - 1)).wait_send()
+
         for k in range(planes):
             copy_gy(w, k).wait_send()
         for k in range(COLUMNS):
@@ -309,7 +353,8 @@
             pltpu.VMEM(estack, f32),
             pltpu.VMEM((others,) + estack, f32),
             dma((loads,)), dma((walkers,)),
-            dma((walkers, others)), dma((walkers, others)),
+            dma((walkers, planes)), dma((walkers, planes)),
+            dma((walkers, planes)), dma((walkers, planes)),
             dma((walkers, planes)), dma((walkers, planes)),
             dma((walkers, COLUMNS)), dma((walkers, COLUMNS)),
             dma((units,)), dma((units,)),

time: 56.3 us -> 63.7 us (1.13)
  Pallas kernels: 53.3 us -> 60.7 us
    pallas_call x1, Pallas kernels: 53.3 us -> 60.7 us  [per_device_kernel(): pl.pallas_call(functools.partial(exchange_kernel, scale), out_shape=(jax....]
where the time goes in v9:
time: 63.7 us; the launch traced here: 63.5 us
  Pallas kernels  60.7 us (95%)
  local copies, waits for them, and re-layouts  1.41 us (2%)
  other arithmetic  0.79 us (1%)
  between operations  0.66 us (1%)
    pallas_call x1, Pallas kernels, per_device_kernel(): pl.pallas_call(functools.partial(exchange_kernel, scale), out_shape=(jax....  60.7 us
    unnamed x5, local copies, waits for them, and re-layouts  1.41 us

profile of v9, /device:TPU:0, one launch (start us, length us, event | category | flops | bytes accessed | tf_op | source)
XLA Modules:
  0.0 63.5 jit_solution(12753422954356545151)
XLA Ops:
  0.6 0.0 copy-start
  0.6 0.9 %copy-done = bf16[4,16,1024]{2,1,0:T(8,128)(2,1)S(1)} copy-done((bf16[4,16,1024]{2,1,0:T(8,128)(2,1)S(1)}, bf16[4,16,1024]{2,1,0:T(8,128)(2,1)}, u32[]{:S(2)}) %copy-start) | copy-done | bytes 131096
  1.5 0.0 copy-start.1
  1.5 60.7 %shard_map.50 = (f32[4]{0:T(128)S(1)}, f32[4,16,1024]{2,1,0:T(8,128)S(1)}) custom-call(bf16[4,16,1024]{2,1,0:T(8,128)(2,1)S(1)} %copy-done, bf16[12,256,1024]{2,1,0:T(8,128)(2,1)} %chol_ref.1), custom_call_target="tpu_custom_call" | custom-call | flops 12884901888 | bytes 6291456 | tf_op jit(solution)/shard_map/pallas_call | solution.py:323
  62.2 0.0 copy-done.1
  62.2 0.8 %broadcast_multiply_fusion = f32[4,16,1024]{2,1,0:T(8,128)} fusion(f32[4,16,1024]{2,1,0:T(8,128)S(1)} %get-tuple-element.5, f32[4]{0:T(128)S(1)} %copy-done.1), kind=kLoop, calls=%fused_computation | loop fusion | flops 65536 | bytes 524304 | tf_op jit(solution)/shard_map/mul | solution.py:375
  63.0 0.5 copy.6
Async XLA Ops:
  0.6 0.9 %copy-start = (bf16[4,16,1024]{2,1,0:T(8,128)(2,1)S(1)}, bf16[4,16,1024]{2,1,0:T(8,128)(2,1)}, u32[]{:S(2)}) copy-start(bf16[4,16,1024]{2,1,0:T(8,128)(2,1)} %green_ref.1) | copy-start | bytes 393220
  1.5 60.7 %copy-start.1 = (f32[4]{0:T(128)S(1)}, f32[4]{0:T(128)}, u32[]{:S(2)}) copy-start(f32[4]{0:T(128)} %param.5) | copy-start | bytes 52

commit v10 on v5

--- a/solution.py
+++ b/solution.py
@@ -38,6 +38,7 @@
     source = [lax.rem(z - k + planes, planes) for k in range(planes)]
     over_z = [device(plane[k], y, c) for k in range(1, planes)]
     over_y = device(z, 1 - y, c)
+    across = [device(plane[k], 1 - y, c) for k in range(1, planes)]
     over_c = device(z, y, 1 - c)
 
     own = [pltpu.make_async_copy(green_ref.at[w], full.at[w, z, y, c], own_sem.at[w]) for w in range(walkers)]
@@ -55,9 +56,9 @@
         load(i).start()
 
     barrier = pltpu.get_barrier_semaphore()
-    for peer in over_z + [over_y, over_c]:
+    for peer in over_z + across + [over_y, over_c]:
         pl.semaphore_signal(barrier, inc=1, device_id=peer, device_id_type=pl.DeviceIdType.MESH)
-    pl.semaphore_wait(barrier, planes + 1)
+    pl.semaphore_wait(barrier, 2 * planes)
 
     def remote(src, dst, send_sem, recv_sem, peer):
         return pltpu.make_async_remote_copy(
@@ -93,11 +94,16 @@
         for k in range(planes - 1, 0, -1):
             copy_gz(w, k).start()
         copy_gy(w, 0).start()
+        if w == 0:
+            block = full.at[w, z, y, c]
+            for k in range(planes - 1, 0, -1):
+                remote(block, block, gy_send.at[w, k], gy_recv.at[w, k], across[k - 1]).start()
 
     def gather_z(w):
         for k in range(1, planes):
             copy_gz(w, k).wait_recv()
-            copy_gy(w, k).start()
+            if type(w) is not int or w > 0:
+                copy_gy(w, k).start()
         copy_gc(w, 0).start()
 
     def gather_y(w):

time: 56.3 us -> 60.1 us (1.067)
  Pallas kernels: 53.3 us -> 57.1 us
    pallas_call x1, Pallas kernels: 53.3 us -> 57.1 us  [per_device_kernel(): pl.pallas_call(functools.partial(exchange_kernel, scale), out_shape=(jax....]
where the time goes in v10:
time: 60.1 us; the launch traced here: 59.9 us
  Pallas kernels  57.1 us (95%)
  local copies, waits for them, and re-layouts  1.41 us (2%)
  other arithmetic  0.79 us (1%)
  between operations  0.66 us (1%)
    pallas_call x1, Pallas kernels, per_device_kernel(): pl.pallas_call(functools.partial(exchange_kernel, scale), out_shape=(jax....  57.1 us
    unnamed x5, local copies, waits for them, and re-layouts  1.41 us

profile of v10, /device:TPU:0, one launch (start us, length us, event | category | flops | bytes accessed | tf_op | source)
XLA Modules:
  0.0 59.9 jit_solution(18269542853547654460)
XLA Ops:
  0.6 0.0 copy-start
  0.6 0.9 %copy-done = bf16[4,16,1024]{2,1,0:T(8,128)(2,1)S(1)} copy-done((bf16[4,16,1024]{2,1,0:T(8,128)(2,1)S(1)}, bf16[4,16,1024]{2,1,0:T(8,128)(2,1)}, u32[]{:S(2)}) %copy-start) | copy-done | bytes 131096
  1.5 0.0 copy-start.1
  1.5 57.1 %shard_map.50 = (f32[4]{0:T(128)S(1)}, f32[4,16,1024]{2,1,0:T(8,128)S(1)}) custom-call(bf16[4,16,1024]{2,1,0:T(8,128)(2,1)S(1)} %copy-done, bf16[12,256,1024]{2,1,0:T(8,128)(2,1)} %chol_ref.1), custom_call_target="tpu_custom_call" | custom-call | flops 12884901888 | bytes 6291456 | tf_op jit(solution)/shard_map/pallas_call | solution.py:285
  58.6 0.0 copy-done.1
  58.6 0.8 %broadcast_multiply_fusion = f32[4,16,1024]{2,1,0:T(8,128)} fusion(f32[4,16,1024]{2,1,0:T(8,128)S(1)} %get-tuple-element.5, f32[4]{0:T(128)S(1)} %copy-done.1), kind=kLoop, calls=%fused_computation | loop fusion | flops 65536 | bytes 524304 | tf_op jit(solution)/shard_map/mul | solution.py:336
  59.4 0.5 copy.6
Async XLA Ops:
  0.6 0.9 %copy-start = (bf16[4,16,1024]{2,1,0:T(8,128)(2,1)S(1)}, bf16[4,16,1024]{2,1,0:T(8,128)(2,1)}, u32[]{:S(2)}) copy-start(bf16[4,16,1024]{2,1,0:T(8,128)(2,1)} %green_ref.1) | copy-start | bytes 393220
  1.5 57.1 %copy-start.1 = (f32[4]{0:T(128)S(1)}, f32[4]{0:T(128)}, u32[]{:S(2)}) copy-start(f32[4]{0:T(128)} %param.5) | copy-start | bytes 52
